TPU v7x, 32 devices: a whole 2x2x4 slice. The times are simulated.
32 devices in a mesh: dp: 4 (over y, x), expert: 8 (over z, core).
Axes of the slice: x: 2, y: 2, z: 4, core: 2. Of those that a mesh axis runs over, the one named last changes fastest.
Arguments:
- patches: bfloat16 [4096, 1024], P(('dp', 'expert')), may hold values from -6 to 6
- expert_ids: int32 [4096, 2], P(('dp', 'expert')), may hold values from 0 to 7, all different within a row; in each aligned block of 128 rows (0 to 127, 128 to 255, ...) at most 64 rows name the same one
- gate_weights: float32 [4096, 2], P(('dp', 'expert')), may hold values from 0.2 to 1
- conv_weight: float32 [49, 1024], replicated, may hold values from -2 to 2
- conv_bias: float32 [1024], replicated, may hold values from -6 to 6
- ln_gain: float32 [1024], replicated, may hold values from 0.1 to 1.9
- ln_shift: float32 [1024], replicated, may hold values from -6 to 6
- w_in: bfloat16 [8, 1024, 1024], P('expert', 'dp'), may hold values from -0.1875 to 0.1875
- w_out: bfloat16 [8, 1024, 1024], P('expert', 'dp'), may hold values from -0.1875 to 0.1875
- grad_mixed: bfloat16 [4096, 1024], P(('dp', 'expert')), may hold values from -6 to 6
Outputs:
- mixed: bfloat16 [4096, 1024], P(('dp', 'expert'))
- grad_input: float32 [4096, 1024], P(('dp', 'expert'))
- grad_w_in: float32 [8, 1024, 1024], P('expert', 'dp')
- grad_w_out: float32 [8, 1024, 1024], P('expert', 'dp')
Inputs may be any that keep to these rules, and one draw needn't show every extreme that they name: `expert_ids`: the two ids of a row differ. Within the 128 rows of one device no expert is named more than 64 times, a bound that some block reaches in every draw.
All inputs are finite; a program needn't handle non-finite values.
Results may differ from a plain program's by a relative error of at most 0.013.
Values may be sent and summed in bfloat16 or wider, within the bound.
A program may use at most 64 MiB of HBM per device.

v0:
```python
from functools import partial

import jax
import jax.numpy as jnp
from jax import lax
from jax.sharding import PartitionSpec as P

KSIZE = 7
TOP = 2
IMG_W = 16
IMG_H = 8


EPS = 1e-06


def front(images, conv_weight, conv_bias, ln_gain, ln_shift):
    half = KSIZE // 2
    padded = jnp.pad(images, ((0, 0), (half, half), (half, half), (0, 0)))
    total = jnp.zeros_like(images) + conv_bias
    for row in range(KSIZE):
        for col in range(KSIZE):
            total = (
                total
                + padded[:, row : row + IMG_H, col : col + IMG_W, :]
                * conv_weight[row * KSIZE + col]
            )
    mean = jnp.mean(total, axis=-1, keepdims=True)
    centred = total - mean
    spread = jnp.mean(centred * centred, axis=-1, keepdims=True)
    return centred * lax.rsqrt(spread + EPS) * ln_gain + ln_shift


def slot_positions(ids, capacity, count):
    flat = ids.reshape(-1)
    table = (flat[:, None] == jnp.arange(count, dtype=jnp.int32)[None, :]).astype(jnp.int32)
    earlier = jnp.cumsum(table, axis=0) - table
    slots = jnp.sum(earlier * table, axis=1)
    return (flat * capacity + slots).reshape(ids.shape)


def contract_last(left, right):
    return lax.dot_general(
        left, right, (((1,), (1,)), ((), ())), preferred_element_type=jnp.float32
    )


def contract_first(left, right):
    return lax.dot_general(
        left, right, (((0,), (0,)), ((), ())), preferred_element_type=jnp.float32
    )


def local(
    patches,
    expert_ids,
    gate_weights,
    conv_weight,
    conv_bias,
    ln_gain,
    ln_shift,
    w_in,
    w_out,
    grad_mixed,
):
    tokens_here = patches.shape[0]
    width = patches.shape[1]
    hid_width = w_in.shape[2]
    experts = lax.axis_size("expert")
    capacity = 4 * tokens_here // experts
    shaped = partial(
        front, conv_weight=conv_weight, conv_bias=conv_bias, ln_gain=ln_gain, ln_shift=ln_shift
    )
    images = patches.astype(jnp.float32).reshape(1, IMG_H, IMG_W, width)
    pre, back_front = jax.vjp(shaped, images)
    normed = pre.reshape(tokens_here, width).astype(jnp.bfloat16)
    positions = slot_positions(expert_ids, capacity, experts)
    all_slots = jnp.arange(experts * capacity, dtype=jnp.int32)
    hits = positions[None, :, :] == all_slots[:, None, None]
    select = jnp.sum(hits.astype(jnp.float32), axis=2).astype(jnp.bfloat16)
    sent = jnp.dot(select, normed, preferred_element_type=jnp.float32).astype(jnp.bfloat16)
    sent = sent.reshape(experts, capacity, width)
    full_in, full_out = (
        lax.all_gather(w_in, "dp", axis=1, tiled=True),
        lax.all_gather(w_out, "dp", axis=1, tiled=True),
    )
    full_in = full_in[0]
    full_out = full_out[0]
    rows = lax.all_to_all(sent, "expert", split_axis=0, concat_axis=0, tiled=True)
    sources = rows.shape[0]
    count = rows.shape[1]
    flat = rows.reshape(sources * count, width)
    hidden_pre = jnp.dot(flat, full_in, preferred_element_type=jnp.float32)
    hidden = jax.nn.gelu(hidden_pre).astype(jnp.bfloat16)
    result = contract_last(hidden, full_out).astype(jnp.bfloat16).reshape(sources, count, width)
    returned = lax.all_to_all(result, "expert", split_axis=0, concat_axis=0, tiled=True)
    returned, received, hidden_pre, hidden = (
        returned,
        rows,
        hidden_pre.reshape(sources, count, hid_width),
        hidden.reshape(sources, count, hid_width),
    )
    back_flat = returned.reshape(experts * capacity, width)
    picked = (
        jnp.take(back_flat, positions.reshape(-1), axis=0)
        .reshape(tokens_here, TOP, width)
        .astype(jnp.float32)
    )
    combined = jnp.sum(picked * gate_weights[:, :, None], axis=1)
    mixed = (patches.astype(jnp.float32) + combined).astype(jnp.bfloat16)
    gated_pairs = (gate_weights[:, :, None] * grad_mixed.astype(jnp.float32)[:, None, :]).astype(
        jnp.bfloat16
    )
    gated_pairs = gated_pairs.reshape(tokens_here * TOP, width)
    pair_select = hits.reshape(experts * capacity, tokens_here * TOP).astype(jnp.bfloat16)
    grad_sent = jnp.dot(pair_select, gated_pairs, preferred_element_type=jnp.float32).astype(
        jnp.bfloat16
    )
    grad_rows = lax.all_to_all(
        grad_sent.reshape(experts, capacity, width),
        "expert",
        split_axis=0,
        concat_axis=0,
        tiled=True,
    )
    row_count = grad_rows.shape[0] * grad_rows.shape[1]
    grad_flat = grad_rows.reshape(row_count, width)
    recv_flat = received.reshape(row_count, width)
    pre_flat = hidden_pre.reshape(row_count, hid_width)
    hidden_flat = hidden.reshape(row_count, hid_width)
    raw = jnp.dot(
        grad_flat,
        lax.all_gather(w_out, "dp", axis=1, tiled=True)[0],
        preferred_element_type=jnp.float32,
    )
    grad_hidden = jax.vjp(jax.nn.gelu, pre_flat)[1](raw)[0].astype(jnp.bfloat16)
    grad_back = contract_last(grad_hidden, lax.all_gather(w_in, "dp", axis=1, tiled=True)[0])
    term_in = contract_first(recv_flat, grad_hidden)
    term_out = contract_first(grad_flat, hidden_flat)
    both_grads = lax.psum_scatter(
        jnp.concatenate([term_in, term_out], axis=1).astype(jnp.bfloat16),
        "dp",
        scatter_dimension=0,
        tiled=True,
    ).astype(jnp.float32)
    grad_w_in = both_grads[:, :hid_width][None]
    grad_w_out = both_grads[:, hid_width:][None]
    grad_back = grad_back.astype(jnp.bfloat16).reshape(
        grad_rows.shape[0], grad_rows.shape[1], width
    )
    grad_returned = lax.all_to_all(grad_back, "expert", split_axis=0, concat_axis=0, tiled=True)
    picked_grad = jnp.take(
        grad_returned.reshape(experts * capacity, width), positions.reshape(-1), axis=0
    )
    grad_normed = jnp.sum(picked_grad.reshape(tokens_here, TOP, width).astype(jnp.float32), axis=1)
    grad_front = back_front(grad_normed.reshape(1, IMG_H, IMG_W, width))[0]
    grad_input = grad_mixed.astype(jnp.float32) + grad_front.reshape(tokens_here, width)
    return (mixed, grad_input, grad_w_in, grad_w_out)


def solution(mesh):
    placed = (
        P(("dp", "expert"), None),
        P(("dp", "expert"), None),
        P(("dp", "expert"), None),
        P(),
        P(),
        P(),
        P(),
        P("expert", "dp", None),
        P("expert", "dp", None),
        P(("dp", "expert"), None),
    )
    return jax.shard_map(
        local,
        mesh=mesh,
        in_specs=placed,
        out_specs=(
            P(("dp", "expert"), None),
            P(("dp", "expert"), None),
            P("expert", "dp", None),
            P("expert", "dp", None),
        ),
        check_vma=False,
    )
```

profile of v0, /device:TPU:0, one launch (start us, length us, event | category | flops | bytes accessed | tf_op | source)
XLA Modules:
  0.0 198.4 jit_solution(13576823674589166515)
XLA Ops:
  7.2 0.7 all-gather.3.cloned.1.call-update
  7.9 0.8 copy.25
  9.0 1.1 fusion.134
  10.1 1.4 fusion.132
  11.6 0.6 reduce-window.6
  12.7 0.7 multiply_add_fusion.1
  13.5 1.3 fusion.133
  14.8 1.0 bitcast_convert_fusion.1
  15.9 5.0 %fusion.130 = (f32[8,16]{1,0:T(8,128)S(1)}, f32[1,8,16,1024]{3,2,1,0:T(8,128)S(1)}) fusion(f32[1024]{0:T(1024)S(1)} %bitcast.186, f32[1024]{0:T(1024)S(1)} %bitcast.132, f32[1024]{0:T(1024)S(1)} %bitcast.150, f32[1024]{0:T(1024)S(1)} %bitcast.190, f32[1024]{0:T(1024)S(1)} %bitcast.192, f32[1024]{0:T(1024)S(1)} %bitcast.194, f32[1024]{0:T(1024)S(1)} %bitcast.196, ...), kind=kLoop, calls=%fused_computation.265 | loop fusion | flops 12976000 | bytes 1253888 | tf_op jit(solution)/shard_map/jvp()/reduce_sum | solution.py:28
  21.8 1.4 convolution_convert_fusion.2
  23.2 6.3 %all-to-all-start = ((bf16[8,64,1024]{2,1,0:T(8,128)(2,1)}), bf16[8,64,1024]{2,1,0:T(8,128)(2,1)S(1)}, u32[]{:S(2)}, u32[]{:S(2)}) async-start(bf16[8,64,1024]{2,1,0:T(8,128)(2,1)} %bitcast.53), calls=%async_computation | async-start | bytes 2097152 | tf_op jit(solution)/shard_map/all_to_all | solution.py:89
  29.6 0.7 all-gather.5.cloned.1.call-update
  30.4 1.5 bitcast_convert_fusion
  31.9 24.3 %all-to-all-done = bf16[8,64,1024]{2,1,0:T(8,128)(2,1)S(1)} async-done(((bf16[8,64,1024]{2,1,0:T(8,128)(2,1)}), bf16[8,64,1024]{2,1,0:T(8,128)(2,1)S(1)}, u32[]{:S(2)}, u32[]{:S(2)}) %all-to-all-start) | async-done | bytes 1048608 | tf_op jit(solution)/shard_map/all_to_all | solution.py:89
  56.2 3.6 %all-to-all-start.2 = ((bf16[8,64,1024]{2,1,0:T(8,128)(2,1)}), bf16[8,64,1024]{2,1,0:T(8,128)(2,1)S(1)}, u32[]{:S(2)}, u32[]{:S(2)}) async-start(bf16[8,64,1024]{2,1,0:T(8,128)(2,1)} %bitcast.60), calls=%async_computation.2 | async-start | bytes 2097152 | tf_op jit(solution)/shard_map/all_to_all | solution.py:119
  60.0 4.2 %fusion.13 = f32[512,1024]{1,0:T(8,128)} fusion(bf16[512,1024]{1,0:T(8,128)(2,1)S(1)} %bitcast.108, bf16[1,1024,1024]{2,1,0:T(8,128)(2,1)} %all-gather.3.cloned.1.call-done), kind=kOutput, calls=%fused_computation.67 | convolution fusion | flops 1073741824 | bytes 5242880 | tf_op jit(solution)/shard_map/dot_general | solution.py:93
  64.2 22.0 %all-to-all-done.2 = bf16[8,64,1024]{2,1,0:T(8,128)(2,1)S(1)} async-done(((bf16[8,64,1024]{2,1,0:T(8,128)(2,1)}), bf16[8,64,1024]{2,1,0:T(8,128)(2,1)S(1)}, u32[]{:S(2)}, u32[]{:S(2)}) %all-to-all-start.2) | async-done | bytes 1048608 | tf_op jit(solution)/shard_map/all_to_all | solution.py:119
  86.3 1.0 copy-done.5
  87.2 3.4 %convolution_convert_fusion = bf16[1024,1024]{0,1:T(8,128)(2,1)S(1)} fusion(bf16[512,1024]{1,0:T(8,128)(2,1)} %bitcast.111, f32[512,1024]{1,0:T(8,128)} %fusion.13), kind=kOutput, calls=%fused_computation.70 | convolution fusion | flops 1079508992 | bytes 5242880 | tf_op jit(solution)/shard_map/dot_general | solution.py:49
  90.7 4.9 %fusion.6 = bf16[512,1024]{1,0:T(8,128)(2,1)S(1)} fusion(f32[512,1024]{1,0:T(8,128)} %fusion.13, bf16[512,1024]{1,0:T(8,128)(2,1)} %bitcast.112, bf16[1,1024,1024]{2,1,0:T(8,128)(2,1)} %all-gather.5.cloned.1.call-done), kind=kOutput, calls=%fused_computation.59 | convolution fusion | flops 1084227584 | bytes 6291456 | tf_op jit(solution)/shard_map/dot_general | solution.py:131
  95.6 1.0 copy-done.46
  96.6 1.3 convolution_convert_fusion.1
  97.9 2.4 %pad_maximum_fusion = bf16[1024,2048]{0,1:T(8,128)(2,1)} fusion(bf16[1024,1024]{0,1:T(8,128)(2,1)S(1)} %convolution_convert_fusion, bf16[1024,1024]{0,1:T(8,128)(2,1)S(1)} %convolution_convert_fusion.1), kind=kLoop, calls=%fused_computation.50 | loop fusion | flops 8388608 | bytes 8388608 | tf_op jit(solution)/shard_map/concatenate | solution.py:141
  100.3 1.6 copy-done.45
  101.9 4.0 %fusion.20 = bf16[512,1024]{1,0:T(8,128)(2,1)} fusion(bf16[1,1024,1024]{2,1,0:T(8,128)(2,1)S(1)} %copy-done.45, f32[512,1024]{1,0:T(8,128)} %fusion.13), kind=kOutput, calls=%fused_computation.74 | convolution fusion | flops 1078984704 | bytes 5242880 | tf_op jit(solution)/shard_map/dot_general | solution.py:43
  105.9 3.7 %all-to-all-start.1 = ((bf16[8,64,1024]{2,1,0:T(8,128)(2,1)}), bf16[8,64,1024]{2,1,0:T(8,128)(2,1)S(1)}, u32[]{:S(2)}, u32[]{:S(2)}) async-start(bf16[8,64,1024]{2,1,0:T(8,128)(2,1)} %bitcast.57), calls=%async_computation.1 | async-start | bytes 2097152 | tf_op jit(solution)/shard_map/all_to_all | solution.py:96
  109.6 3.8 %fusion.17 = bf16[512,1024]{1,0:T(8,128)(2,1)} fusion(bf16[512,1024]{1,0:T(8,128)(2,1)S(1)} %copy-done.47, bf16[1,1024,1024]{2,1,0:T(8,128)(2,1)} %all-gather.3.cloned.1.call-done), kind=kOutput, calls=%fused_computation.73 | convolution fusion | flops 1074266112 | bytes 4194304 | tf_op jit(solution)/shard_map/dot_general | solution.py:43
  113.4 22.7 %all-to-all-done.1 = bf16[8,64,1024]{2,1,0:T(8,128)(2,1)S(1)} async-done(((bf16[8,64,1024]{2,1,0:T(8,128)(2,1)}), bf16[8,64,1024]{2,1,0:T(8,128)(2,1)S(1)}, u32[]{:S(2)}, u32[]{:S(2)}) %all-to-all-start.1) | async-done | bytes 1048608 | tf_op jit(solution)/shard_map/all_to_all | solution.py:96
  136.1 3.8 %all-to-all-start.3 = ((bf16[8,64,1024]{2,1,0:T(8,128)(2,1)}), bf16[8,64,1024]{2,1,0:T(8,128)(2,1)S(1)}, u32[]{:S(2)}, u32[]{:S(2)}) async-start(bf16[8,64,1024]{2,1,0:T(8,128)(2,1)} %bitcast.110), calls=%async_computation.3 | async-start | bytes 2097152 | tf_op jit(solution)/shard_map/all_to_all | solution.py:151
  139.9 0.5 compare_and_fusion
  140.4 0.6 pad_clamp_fusion
  141.0 1.3 gather_fusion
  142.3 23.9 %all-to-all-done.3 = bf16[8,64,1024]{2,1,0:T(8,128)(2,1)S(1)} async-done(((bf16[8,64,1024]{2,1,0:T(8,128)(2,1)}), bf16[8,64,1024]{2,1,0:T(8,128)(2,1)S(1)}, u32[]{:S(2)}, u32[]{:S(2)}) %all-to-all-start.3) | async-done | bytes 1048608 | tf_op jit(solution)/shard_map/all_to_all | solution.py:151
  166.2 2.1 %gather_fusion.1 = bf16[256,1024]{1,0:T(8,128)(2,1)} fusion(bf16[512,1024]{1,0:T(8,128)(2,1)S(1)} %bitcast.105, s32[1024]{0:T(1024)} %pad_clamp_fusion), kind=kCustom, calls=%fused_computation.1.clone | custom fusion | bytes 1049600 | tf_op jit(solution)/shard_map/jit(_take)/gather | solution.py:152
  168.3 1.2 select_convert_fusion
  169.5 1.6 reshape.335
  171.1 1.6 reshape.334
  172.7 1.2 reduce_sum.88
  174.3 1.6 fusion.23
  176.6 0.8 broadcast_multiply_fusion.3
  177.4 1.2 broadcast_multiply_fusion.2
  178.7 1.2 broadcast_multiply_fusion.1
  179.9 5.8 %pad_add_fusion = f32[1,14,22,1024]{3,2,1,0:T(8,128)S(1)} fusion(f32[1,8,16,1024]{3,2,1,0:T(8,128)S(1)} %get-tuple-element.31, f32[1,8,16,1024]{3,2,1,0:T(8,128)S(1)} %get-tuple-element.32, f32[1,8,16,1024]{3,2,1,0:T(8,128)S(1)} %get-tuple-element.33, f32[1,8,16,1024]{3,2,1,0:T(8,128)S(1)} %get-tuple-element.34, ...), kind=kLoop, calls=%fused_computation.75 | loop fusion | flops 13246464 | bytes 23805952 | tf_op jit(solution)/shard_map/transpose(jvp())/add_any | solution.py:25
  186.1 0.6 copy-done.1
  186.7 1.0 bitcast_add_fusion
  187.7 1.4 convert_element_type.90
  189.2 1.3 copy.30
  190.6 1.3 copy.29
  (121 shorter events, 3.5 us)
Async XLA Ops:
  7.2 8.7 %copy-start.41 = (f32[1024]{0:T(1024)S(1)}, f32[1024]{0:T(1024)}, u32[]{:S(2)}) copy-start(f32[1024]{0:T(1024)} %param.16) | copy-start | bytes 12292
  7.2 14.5 %copy-start.6 = (f32[1024]{0:T(1024)S(1)}, f32[1024]{0:T(1024)}, u32[]{:S(2)}) copy-start(f32[1024]{0:T(1024)} %param.17) | copy-start | bytes 12292
  7.2 14.5 %copy-start.42 = (f32[1024]{0:T(1024)S(1)}, f32[1024]{0:T(1024)}, u32[]{:S(2)}) copy-start(f32[1024]{0:T(1024)} %param.18) | copy-start | bytes 12292
  7.2 52.8 %all-gather.3.cloned.1.call-start = ((), (), s32[]{:S(2)}) async-start(), calls=%async_computation.5 | async-start | bytes 2621440 | tf_op jit(solution)/shard_map/all_gather | solution.py:84
  10.1 11.0 %copy-start.13 = (f32[1,1024]{1,0:T(1,128)}, f32[1,1024]{1,0:T(1,128)S(1)}, u32[]{:S(2)}) copy-start(f32[1,1024]{1,0:T(1,128)S(1)} %get-tuple-element.120) | copy-start | bytes 12292
  11.4 9.4 %copy-start.17 = (f32[1,1024]{1,0:T(1,128)}, f32[1,1024]{1,0:T(1,128)S(1)}, u32[]{:S(2)}) copy-start(f32[1,1024]{1,0:T(1,128)S(1)} %get-tuple-element.73) | copy-start | bytes 12292
  11.4 9.6 %copy-start.19 = (f32[1,1024]{1,0:T(1,128)}, f32[1,1024]{1,0:T(1,128)S(1)}, u32[]{:S(2)}) copy-start(f32[1,1024]{1,0:T(1,128)S(1)} %get-tuple-element.75) | copy-start | bytes 12292
  11.5 9.6 %copy-start.21 = (f32[1,1024]{1,0:T(1,128)}, f32[1,1024]{1,0:T(1,128)S(1)}, u32[]{:S(2)}) copy-start(f32[1,1024]{1,0:T(1,128)S(1)} %get-tuple-element.76) | copy-start | bytes 12292
  11.5 9.6 %copy-start.23 = (f32[1,1024]{1,0:T(1,128)}, f32[1,1024]{1,0:T(1,128)S(1)}, u32[]{:S(2)}) copy-start(f32[1,1024]{1,0:T(1,128)S(1)} %get-tuple-element.77) | copy-start | bytes 12292
  11.5 9.6 %copy-start.25 = (f32[1,1024]{1,0:T(1,128)}, f32[1,1024]{1,0:T(1,128)S(1)}, u32[]{:S(2)}) copy-start(f32[1,1024]{1,0:T(1,128)S(1)} %get-tuple-element.78) | copy-start | bytes 12292
  11.5 9.6 %copy-start.27 = (f32[1,1024]{1,0:T(1,128)}, f32[1,1024]{1,0:T(1,128)S(1)}, u32[]{:S(2)}) copy-start(f32[1,1024]{1,0:T(1,128)S(1)} %get-tuple-element.79) | copy-start | bytes 12292
  11.5 9.6 %copy-start.29 = (f32[1,1024]{1,0:T(1,128)}, f32[1,1024]{1,0:T(1,128)S(1)}, u32[]{:S(2)}) copy-start(f32[1,1024]{1,0:T(1,128)S(1)} %get-tuple-element.80) | copy-start | bytes 12292
  11.5 9.6 %copy-start.31 = (f32[1,1024]{1,0:T(1,128)}, f32[1,1024]{1,0:T(1,128)S(1)}, u32[]{:S(2)}) copy-start(f32[1,1024]{1,0:T(1,128)S(1)} %get-tuple-element.81) | copy-start | bytes 12292
  11.5 9.6 %copy-start.33 = (f32[1,1024]{1,0:T(1,128)}, f32[1,1024]{1,0:T(1,128)S(1)}, u32[]{:S(2)}) copy-start(f32[1,1024]{1,0:T(1,128)S(1)} %get-tuple-element.82) | copy-start | bytes 12292
  11.5 9.6 %copy-start.35 = (f32[1,1024]{1,0:T(1,128)}, f32[1,1024]{1,0:T(1,128)S(1)}, u32[]{:S(2)}) copy-start(f32[1,1024]{1,0:T(1,128)S(1)} %get-tuple-element.83) | copy-start | bytes 12292
  11.5 9.6 %copy-start.37 = (f32[1,1024]{1,0:T(1,128)}, f32[1,1024]{1,0:T(1,128)S(1)}, u32[]{:S(2)}) copy-start(f32[1,1024]{1,0:T(1,128)S(1)} %get-tuple-element.84) | copy-start | bytes 12292
  11.5 9.6 %copy-start.39 = (f32[1,1024]{1,0:T(1,128)}, f32[1,1024]{1,0:T(1,128)S(1)}, u32[]{:S(2)}) copy-start(f32[1,1024]{1,0:T(1,128)S(1)} %get-tuple-element.85) | copy-start | bytes 12292
  14.8 6.0 %copy-start.7 = (f32[1,1024]{1,0:T(1,128)}, f32[1,1024]{1,0:T(1,128)S(1)}, u32[]{:S(2)}) copy-start(f32[1,1024]{1,0:T(1,128)S(1)} %get-tuple-element.101) | copy-start | bytes 12292
  14.8 8.4 %copy-start.9 = (f32[1,1024]{1,0:T(1,128)}, f32[1,1024]{1,0:T(1,128)S(1)}, u32[]{:S(2)}) copy-start(f32[1,1024]{1,0:T(1,128)S(1)} %get-tuple-element.102) | copy-start | bytes 12292
  14.8 8.4 %copy-start.11 = (f32[1,1024]{1,0:T(1,128)}, f32[1,1024]{1,0:T(1,128)S(1)}, u32[]{:S(2)}) copy-start(f32[1,1024]{1,0:T(1,128)S(1)} %get-tuple-element.103) | copy-start | bytes 12292
  21.8 8.5 %copy-start.2 = (bf16[128,1024]{1,0:T(8,128)(2,1)S(1)}, bf16[128,1024]{1,0:T(8,128)(2,1)}, u32[]{:S(2)}) copy-start(bf16[128,1024]{1,0:T(8,128)(2,1)} %param.21) | copy-start | bytes 786436
  21.8 8.5 %copy-start.43 = (f32[128,2]{0,1:T(2,128)S(1)}, f32[128,2]{0,1:T(2,128)}, u32[]{:S(2)}) copy-start(f32[128,2]{0,1:T(2,128)} %param.14) | copy-start | bytes 3076
  23.2 32.9 %all-to-all-start = ((bf16[8,64,1024]{2,1,0:T(8,128)(2,1)}), bf16[8,64,1024]{2,1,0:T(8,128)(2,1)S(1)}, u32[]{:S(2)}, u32[]{:S(2)}) async-start(bf16[8,64,1024]{2,1,0:T(8,128)(2,1)} %bitcast.53), calls=%async_computation | async-start | bytes 2097152 | tf_op jit(solution)/shard_map/all_to_all | solution.py:89
  29.6 61.1 %all-gather.5.cloned.1.call-start = ((), (), s32[]{:S(2)}) async-start(), calls=%async_computation.6 | async-start | bytes 2621440 | tf_op jit(solution)/shard_map/all_gather | solution.py:85
  56.2 8.0 %copy-start.3 = (bf16[8,64,1024]{2,1,0:T(8,128)(2,1)}, bf16[8,64,1024]{2,1,0:T(8,128)(2,1)S(1)}, u32[]{:S(2)}) copy-start(bf16[8,64,1024]{2,1,0:T(8,128)(2,1)S(1)} %all-to-all-done) | copy-start | bytes 3145732
  56.2 30.1 %all-to-all-start.2 = ((bf16[8,64,1024]{2,1,0:T(8,128)(2,1)}), bf16[8,64,1024]{2,1,0:T(8,128)(2,1)S(1)}, u32[]{:S(2)}, u32[]{:S(2)}) async-start(bf16[8,64,1024]{2,1,0:T(8,128)(2,1)} %bitcast.60), calls=%async_computation.2 | async-start | bytes 2097152 | tf_op jit(solution)/shard_map/all_to_all | solution.py:119
  59.7 128.0 %reduce-scatter.2.cloned.1.call-start = ((), (), s32[]{:S(2)}) async-start(), calls=%async_computation.7 | async-start | bytes 5242880 | tf_op jit(solution)/shard_map/reduce_scatter | solution.py:140
  90.7 5.9 %copy-start.4 = (bf16[8,64,1024]{2,1,0:T(8,128)(2,1)S(1)}, bf16[8,64,1024]{2,1,0:T(8,128)(2,1)}, u32[]{:S(2)}) copy-start(bf16[8,64,1024]{2,1,0:T(8,128)(2,1)} %copy-done.3) | copy-start | bytes 3145732
  100.3 1.6 copy-start.45
  105.9 3.7 %copy-start.47 = (bf16[512,1024]{1,0:T(8,128)(2,1)S(1)}, bf16[512,1024]{1,0:T(8,128)(2,1)}, u32[]{:S(2)}) copy-start(bf16[512,1024]{1,0:T(8,128)(2,1)} %copy-done.46) | copy-start | bytes 3145732
  105.9 30.2 %all-to-all-start.1 = ((bf16[8,64,1024]{2,1,0:T(8,128)(2,1)}), bf16[8,64,1024]{2,1,0:T(8,128)(2,1)S(1)}, u32[]{:S(2)}, u32[]{:S(2)}) async-start(bf16[8,64,1024]{2,1,0:T(8,128)(2,1)} %bitcast.57), calls=%async_computation.1 | async-start | bytes 2097152 | tf_op jit(solution)/shard_map/all_to_all | solution.py:96
  136.1 30.1 %all-to-all-start.3 = ((bf16[8,64,1024]{2,1,0:T(8,128)(2,1)}), bf16[8,64,1024]{2,1,0:T(8,128)(2,1)S(1)}, u32[]{:S(2)}, u32[]{:S(2)}) async-start(bf16[8,64,1024]{2,1,0:T(8,128)(2,1)} %bitcast.110), calls=%async_computation.3 | async-start | bytes 2097152 | tf_op jit(solution)/shard_map/all_to_all | solution.py:151
  171.1 1.6 copy-start
  171.1 3.0 %copy-start.44 = (f32[128,2]{0,1:T(2,128)S(1)}, f32[128,2]{0,1:T(2,128)}, u32[]{:S(2)}) copy-start(f32[128,2]{0,1:T(2,128)} %param.14) | copy-start | bytes 3076
  172.7 3.2 %copy-start.16 = (f32[8,16]{1,0:T(8,128)S(1)}, f32[8,16]{1,0:T(8,128)}, u32[]{:S(2)}) copy-start(f32[8,16]{1,0:T(8,128)} %copy-done.15) | copy-start | bytes 1540
  174.0 2.2 %copy-start.14 = (f32[1,1024]{1,0:T(1,128)S(1)}, f32[1,1024]{1,0:T(1,128)}, u32[]{:S(2)}) copy-start(f32[1,1024]{1,0:T(1,128)} %copy-done.13) | copy-start | bytes 12292
  174.2 2.3 %copy-start.18 = (f32[1,1024]{1,0:T(1,128)S(1)}, f32[1,1024]{1,0:T(1,128)}, u32[]{:S(2)}) copy-start(f32[1,1024]{1,0:T(1,128)} %copy-done.17) | copy-start | bytes 12292
  174.2 2.3 %copy-start.20 = (f32[1,1024]{1,0:T(1,128)S(1)}, f32[1,1024]{1,0:T(1,128)}, u32[]{:S(2)}) copy-start(f32[1,1024]{1,0:T(1,128)} %copy-done.19) | copy-start | bytes 12292
  174.2 2.3 %copy-start.22 = (f32[1,1024]{1,0:T(1,128)S(1)}, f32[1,1024]{1,0:T(1,128)}, u32[]{:S(2)}) copy-start(f32[1,1024]{1,0:T(1,128)} %copy-done.21) | copy-start | bytes 12292
  174.2 2.3 %copy-start.24 = (f32[1,1024]{1,0:T(1,128)S(1)}, f32[1,1024]{1,0:T(1,128)}, u32[]{:S(2)}) copy-start(f32[1,1024]{1,0:T(1,128)} %copy-done.23) | copy-start | bytes 12292
  174.2 2.3 %copy-start.26 = (f32[1,1024]{1,0:T(1,128)S(1)}, f32[1,1024]{1,0:T(1,128)}, u32[]{:S(2)}) copy-start(f32[1,1024]{1,0:T(1,128)} %copy-done.25) | copy-start | bytes 12292
  174.2 2.3 %copy-start.28 = (f32[1,1024]{1,0:T(1,128)S(1)}, f32[1,1024]{1,0:T(1,128)}, u32[]{:S(2)}) copy-start(f32[1,1024]{1,0:T(1,128)} %copy-done.27) | copy-start | bytes 12292
  174.2 2.3 %copy-start.30 = (f32[1,1024]{1,0:T(1,128)S(1)}, f32[1,1024]{1,0:T(1,128)}, u32[]{:S(2)}) copy-start(f32[1,1024]{1,0:T(1,128)} %copy-done.29) | copy-start | bytes 12292
  174.2 2.3 %copy-start.32 = (f32[1,1024]{1,0:T(1,128)S(1)}, f32[1,1024]{1,0:T(1,128)}, u32[]{:S(2)}) copy-start(f32[1,1024]{1,0:T(1,128)} %copy-done.31) | copy-start | bytes 12292
  174.3 2.3 %copy-start.34 = (f32[1,1024]{1,0:T(1,128)S(1)}, f32[1,1024]{1,0:T(1,128)}, u32[]{:S(2)}) copy-start(f32[1,1024]{1,0:T(1,128)} %copy-done.33) | copy-start | bytes 12292
  174.3 2.3 %copy-start.36 = (f32[1,1024]{1,0:T(1,128)S(1)}, f32[1,1024]{1,0:T(1,128)}, u32[]{:S(2)}) copy-start(f32[1,1024]{1,0:T(1,128)} %copy-done.35) | copy-start | bytes 12292
  174.3 2.3 %copy-start.38 = (f32[1,1024]{1,0:T(1,128)S(1)}, f32[1,1024]{1,0:T(1,128)}, u32[]{:S(2)}) copy-start(f32[1,1024]{1,0:T(1,128)} %copy-done.37) | copy-start | bytes 12292
  174.3 2.3 %copy-start.40 = (f32[1,1024]{1,0:T(1,128)S(1)}, f32[1,1024]{1,0:T(1,128)}, u32[]{:S(2)}) copy-start(f32[1,1024]{1,0:T(1,128)} %copy-done.39) | copy-start | bytes 12292
  (7 other events, 6.0 us)
Sparse Core Ops, SparseCore 0:
  9.9 38.0 all-gather.2
  49.8 35.2 all-gather.4
  100.4 51.5 reduce-scatter.1
where the time goes:
time: 199 us; the launch traced here: 198 us
  waiting for transfers between devices  94.3 us (47%)
  other arithmetic  28 us (14%)
  matrix products  24.6 us (12%)
  local copies, waits for them, and re-layouts  19.3 us (10%)
  starting transfers between devices  17.7 us (9%)
  between operations  14.6 us (7%)
    all_to_all x1, waiting for transfers between devices, local(): lax.all_to_all(sent, 'expert', split_axis=0, concat_axis=0, tiled=True)  24.3 us
    all_to_all x1, waiting for transfers between devices, local(): lax.all_to_all(grad_back, 'expert', split_axis=0, concat_axis=0, tiled=True)  23.9 us
    all_to_all x1, waiting for transfers between devices, local(): lax.all_to_all(result, 'expert', split_axis=0, concat_axis=0, tiled=True)  22.7 us
    all_to_all x1, waiting for transfers between devices, local(): lax.all_to_all(grad_sent.reshape(experts, capacity, width), 'expert', spl...  22 us
    unnamed x99, local copies, waits for them, and re-layouts  8.17 us
    dot_general x2, matrix products, contract_last(): lax.dot_general(left, right, (((1,), (1,)), ((), ())), preferred_element_...  7.85 us
    all_to_all x1, starting transfers between devices, local(): lax.all_to_all(sent, 'expert', split_axis=0, concat_axis=0, tiled=True)  6.33 us
    add_any x2, other arithmetic, front(): padded[:, row:row + IMG_H, col:col + IMG_W, :]  6.13 us
  transfers between devices with their start and end apart: 7, of which 4 were waited for; matrix products, arithmetic and copies ran while one was open for 27% of the time, Pallas kernels for 0%

commit v1 on v0

v1 whole, which is shorter than its diff:
```python
import functools

import jax
import jax.numpy as jnp
from jax import lax
from jax.experimental import pallas as pl
from jax.experimental.pallas import tpu as pltpu
from jax.sharding import PartitionSpec as P

KSIZE = 7
HALF = KSIZE // 2
TOP = 2
IMG_W = 16
IMG_H = 8
EPS = 1e-06
EDGE = 8
MESH = pl.DeviceIdType.MESH
BF = jnp.bfloat16
F32 = jnp.float32


def conv_into(pad, weight_ref, out_ref, bias_ref, flip):
    width = out_ref.shape[1]

    def chunk(i, carry):
        lanes = pl.ds(pl.multiple_of(i * 128, 128), 128)
        total = jnp.zeros((IMG_H, IMG_W, 128), F32)
        if bias_ref is not None:
            total = total + bias_ref[0:1, lanes].reshape(1, 1, 128)
        for col in range(KSIZE):
            start = EDGE - HALF + col
            slab = pad[:, start : start + IMG_W, lanes]
            for row in range(KSIZE):
                tap = row * KSIZE + col
                if flip:
                    tap = KSIZE * KSIZE - 1 - tap
                total = total + slab[row : row + IMG_H] * weight_ref[tap : tap + 1, lanes].reshape(
                    1, 1, 128
                )
        out_ref[:, lanes] = total.reshape(IMG_H * IMG_W, 128)
        return carry

    lax.fori_loop(0, width // 128, chunk, 0)


def fill_pad(pad, image):
    pad[...] = jnp.zeros_like(pad)
    pad[HALF : HALF + IMG_H, EDGE : EDGE + IMG_W, :] = image.reshape(IMG_H, IMG_W, image.shape[-1])


def front_body(patches_ref, weight_ref, bias_ref, gain_ref, shift_ref, conv_ref, normed_ref, pad):
    fill_pad(pad, patches_ref[...].astype(F32))
    conv_into(pad, weight_ref, conv_ref, bias_ref, False)
    conv = conv_ref[...]
    centred = conv - jnp.mean(conv, axis=1, keepdims=True)
    spread = jnp.mean(centred * centred, axis=1, keepdims=True)
    normed_ref[...] = (centred * lax.rsqrt(spread + EPS) * gain_ref[...] + shift_ref[...]).astype(
        BF
    )


def back_body(conv_ref, weight_ref, gain_ref, grad_ref, cot_ref, out_ref, pad):
    conv = conv_ref[...]
    centred = conv - jnp.mean(conv, axis=1, keepdims=True)
    spread = jnp.mean(centred * centred, axis=1, keepdims=True)
    scale = lax.rsqrt(spread + EPS)
    unit = centred * scale
    slope = grad_ref[...] * gain_ref[...]
    inner = slope - jnp.mean(slope, axis=1, keepdims=True)
    inner = inner - unit * jnp.mean(slope * unit, axis=1, keepdims=True)
    fill_pad(pad, inner * scale)
    conv_into(pad, weight_ref, out_ref, None, True)
    out_ref[...] += cot_ref[...].astype(F32)


def dot(left, right, dims):
    return lax.dot_general(left, right, (dims, ((), ())), preferred_element_type=F32)


NN = ((1,), (0,))
NT = ((1,), (1,))
TN = ((0,), (0,))


def moe_body(
    n_dp,
    n_exp,
    cap,
    normed_ref,
    cot_ref,
    meta_ref,
    pos_ref,
    gate_ref,
    patches_ref,
    w_in_ref,
    w_out_ref,
    mixed_ref,
    grad_normed_ref,
    gw_in_ref,
    gw_out_ref,
    win,
    wout,
    all_n,
    all_c,
    all_m,
    rows,
    grads,
    slope,
    hidden,
    ghid,
    outs,
    back,
    r_outs,
    r_back,
    part_in,
    part_out,
    r_in,
    r_out,
    w_send,
    w_recv,
    m_send,
    m_recv,
    line_send,
    line_recv,
    twin_send,
    twin_recv,
    ret_send,
    ret_recv,
    g_send,
    g_recv,
):
    dp = lax.axis_index("dp")
    ex = lax.axis_index("expert")
    chips = n_exp // 2
    chip = ex // 2
    core = ex % 2
    depth = w_in_ref.shape[0]
    width = normed_ref.shape[1]
    hid = w_in_ref.shape[1]
    count = n_exp * cap
    tile = 256

    barrier = pltpu.get_barrier_semaphore()
    for i in range(1, n_exp):
        pl.semaphore_signal(
            barrier, inc=1, device_id=(dp, (ex + i) % n_exp), device_id_type=MESH
        )
    for i in range(1, n_dp):
        pl.semaphore_signal(barrier, inc=1, device_id=((dp + i) % n_dp, ex), device_id_type=MESH)
    pl.semaphore_wait(barrier, n_exp - 1 + n_dp - 1)

    def remote(src, dst, send, recv, to):
        return pltpu.make_async_remote_copy(
            src_ref=src, dst_ref=dst, send_sem=send, recv_sem=recv, device_id=to, device_id_type=MESH
        )

    mine = pl.ds(pl.multiple_of(dp * depth, 16), depth)

    metas = []
    for i in range(1, n_exp):
        copy = remote(
            meta_ref, all_m.at[ex], m_send.at[i], m_recv.at[i], (dp, (ex + i) % n_exp)
        )
        copy.start()
        metas.append(copy)

    own = (normed_ref, cot_ref)
    held = (all_n, all_c)

    def line(a, way, k, src_dev, src):
        step = 1 if way == 0 else -1
        return remote(
            src,
            held[a].at[src_dev],
            line_send.at[a, way, k],
            line_recv.at[a, way, k],
            (dp, jnp.clip(ex + 2 * step, core, n_exp - 2 + core)),
        )

    def twin(a, way, k, src_dev, src):
        return remote(
            src,
            held[a].at[src_dev],
            twin_send.at[a, way, k],
            twin_recv.at[a, way, k],
            (dp, 2 * chip + 1 - core),
        )

    def each(way, k):
        if way == 0:
            return chip - k >= 0, chip + 1 < chips, ex - 2 * k
        return chip + k < chips, chip - 1 >= 0, ex + 2 * k

    def send_step(a, k):
        for way in range(2):
            there, ahead, src_dev = each(way, k)
            src_dev = jnp.clip(src_dev, 0, n_exp - 1)
            src = own[a] if k == 0 else held[a].at[src_dev]
            if k > 0:

                @pl.when(there)
                def _(a=a, way=way, k=k, src_dev=src_dev, src=src):
                    line(a, way, k - 1, src_dev, src).wait_recv()
                    twin(a, way, k, src_dev, src).start()

            if k < chips - 1:

                @pl.when(jnp.logical_and(there, ahead))
                def _(a=a, way=way, k=k, src_dev=src_dev, src=src):
                    line(a, way, k, src_dev, src).start()

            if k == 0 and way == 0:
                twin(a, way, k, src_dev, src).start()

    def finish_twins(a):
        for k in range(chips):
            for way in range(2):
                if k == 0 and way == 1:
                    continue
                there, _, src_dev = each(way, k)
                other = jnp.clip(src_dev + 1 - 2 * core, 0, n_exp - 1)

                @pl.when(there)
                def _(a=a, way=way, k=k, other=other):
                    twin(a, way, k, other, held[a].at[other]).wait_recv()

    def finish_sends(a):
        for k in range(chips):
            for way in range(2):
                there, ahead, src_dev = each(way, k)
                src_dev = jnp.clip(src_dev, 0, n_exp - 1)
                if k < chips - 1:

                    @pl.when(jnp.logical_and(there, ahead))
                    def _(a=a, way=way, k=k, src_dev=src_dev):
                        line(a, way, k, src_dev, own[a]).wait_send()

                if k > 0 or way == 0:

                    @pl.when(there)
                    def _(a=a, way=way, k=k, src_dev=src_dev):
                        twin(a, way, k, src_dev, own[a]).wait_send()

    send_step(0, 0)
    weights = []
    for a, (src, dst) in enumerate(((w_in_ref, win), (w_out_ref, wout))):
        for i in range(1, n_dp):
            copy = remote(
                src, dst.at[mine], w_send.at[a, i], w_recv.at[a, i], ((dp + i) % n_dp, ex)
            )
            copy.start()
            weights.append(copy)
    send_step(1, 0)
    win[mine] = w_in_ref[...]
    wout[mine] = w_out_ref[...]
    all_n[ex] = normed_ref[...]
    all_c[ex] = cot_ref[...]
    all_m[ex] = meta_ref[...]
    for k in range(1, chips):
        send_step(0, k)
        send_step(1, k)
    for copy in metas:
        copy.wait()

    tokens = normed_ref.shape[0]
    slots = lax.broadcasted_iota(jnp.int32, (cap, tokens), 0).astype(F32) + (ex * cap).astype(F32)

    def choose(j):
        info = all_m[j]
        first = jnp.where(slots == info[0:1, :], 1.0, 0.0)
        second = jnp.where(slots == info[1:2, :], 1.0, 0.0)
        gate = jnp.sum(first * info[2:3, :] + second * info[3:4, :], axis=1, keepdims=True)
        return (first + second).astype(BF), gate

    finish_twins(0)

    def gather_rows(j, carry):
        select, _ = choose(j)
        at = pl.ds(pl.multiple_of(j * cap, 16), cap)
        rows[at] = dot(select, all_n[j], NN).astype(BF)
        return carry

    lax.fori_loop(0, n_exp, gather_rows, 0)
    for copy in weights[: n_dp - 1]:
        copy.wait()

    def up(n, carry):
        cols = pl.ds(pl.multiple_of(n * tile, tile), tile)
        x = dot(rows[...], win[:, cols], NN)
        c = 0.7978845608028654
        t = jnp.tanh(c * (x + 0.044715 * (x * x * x)))
        half = 0.5 * (1.0 + t)
        hidden[:, cols] = (x * half).astype(BF)
        slope[:, cols] = half + 0.5 * x * (1.0 - t * t) * (c * (1.0 + 3 * 0.044715 * (x * x)))
        return carry

    lax.fori_loop(0, hid // tile, up, 0)

    finish_twins(1)

    def gather_grads(j, carry):
        select, gate = choose(j)
        at = pl.ds(pl.multiple_of(j * cap, 16), cap)
        grads[at] = (dot(select, all_c[j], NN) * gate).astype(BF)
        return carry

    lax.fori_loop(0, n_exp, gather_grads, 0)
    for copy in weights[n_dp - 1 :]:
        copy.wait()

    def down(n, carry):
        cols = pl.ds(pl.multiple_of(n * tile, tile), tile)
        outs[:, cols] = dot(hidden[...], wout[cols, :], NT).astype(BF)
        return carry

    lax.fori_loop(0, width // tile, down, 0)

    my_rows = pl.ds(pl.multiple_of(ex * cap, 16), cap)

    def give_back(a, src, dst):
        copies = []
        for i in range(1, n_exp):
            to = (ex + i) % n_exp
            copy = remote(
                src.at[pl.ds(pl.multiple_of(to * cap, 16), cap)],
                dst.at[my_rows],
                ret_send.at[a, i],
                ret_recv.at[a, i],
                (dp, to),
            )
            copy.start()
            copies.append(copy)
        dst[my_rows] = src[my_rows]
        return copies

    outs_back = give_back(0, outs, r_outs)

    def down_grad(n, carry):
        cols = pl.ds(pl.multiple_of(n * tile, tile), tile)
        ghid[:, cols] = (dot(grads[...], wout[:, cols], NN) * slope[:, cols]).astype(BF)
        return carry

    lax.fori_loop(0, hid // tile, down_grad, 0)

    def up_grad(n, carry):
        cols = pl.ds(pl.multiple_of(n * tile, tile), tile)
        back[:, cols] = dot(ghid[...], win[cols, :], NT).astype(BF)
        return carry

    lax.fori_loop(0, width // tile, up_grad, 0)
    grads_back = give_back(1, back, r_back)

    shares = []

    def weight_grad(a, left, right, part, got):
        for i in range(1, n_dp + 1):
            to = (dp + i) % n_dp
            cols = pl.ds(pl.multiple_of(to * depth, depth), depth) if depth % 128 == 0 else None
            if cols is None:
                break
            part[to] = dot(left[:, cols], right[...], TN).astype(BF)
            if i < n_dp:
                share(a, i, to, part, got)

    def share(a, i, to, part, got):
        copy = remote(part.at[to], got.at[dp], g_send.at[a, i], g_recv.at[a, i], (to, ex))
        copy.start()
        shares.append(copy)

    def weight_grad_wide(a, left, right, part, got):
        def some(n, carry):
            cols = pl.ds(pl.multiple_of(n * tile, tile), tile)
            made = dot(left[:, cols], right[...], TN).astype(BF)
            each_tile = tile // depth
            part[pl.ds(n * each_tile, each_tile)] = made.reshape(each_tile, depth, hid)
            return carry

        lax.fori_loop(0, width // tile, some, 0)
        for i in range(1, n_dp):
            share(a, i, (dp + i) % n_dp, part, got)

    make = weight_grad if depth % 128 == 0 else weight_grad_wide
    make(0, rows, ghid, part_in, r_in)
    make(1, grads, hidden, part_out, r_out)

    wide = lax.broadcasted_iota(jnp.int32, (tokens, count), 1)
    picks = [wide == pos_ref[:, k : k + 1] for k in range(TOP)]
    ones = [jnp.where(pick, 1.0, 0.0).astype(BF) for pick in picks]
    for copy in outs_back:
        copy.wait()
    total = patches_ref[...].astype(F32)
    combined = dot(ones[0], r_outs[...], NN) * gate_ref[:, 0:1]
    for k in range(1, TOP):
        combined = combined + dot(ones[k], r_outs[...], NN) * gate_ref[:, k : k + 1]
    mixed_ref[...] = (total + combined).astype(BF)
    for copy in grads_back:
        copy.wait()
    both = ones[0]
    for k in range(1, TOP):
        both = both + ones[k]
    grad_normed_ref[...] = dot(both, r_back[...], NN)

    for copy in shares:
        copy.wait()
    for part, got, out in ((part_in, r_in, gw_in_ref), (part_out, r_out, gw_out_ref)):
        value = part[dp].astype(F32)
        for i in range(1, n_dp):
            value = value + got[(dp + i) % n_dp].astype(F32)
        out[...] = value
    finish_sends(0)
    finish_sends(1)


def local(
    patches,
    expert_ids,
    gate_weights,
    conv_weight,
    conv_bias,
    ln_gain,
    ln_shift,
    w_in,
    w_out,
    grad_mixed,
):
    tokens, width = patches.shape
    depth, hid = w_in.shape[1:]
    n_exp = lax.axis_size("expert")
    n_dp = lax.axis_size("dp")
    cap = 4 * tokens // n_exp
    count = n_exp * cap
    bias, gain, shift = conv_bias[None], ln_gain[None], ln_shift[None]
    vmem = pl.BlockSpec(memory_space=pltpu.VMEM)
    pad = pltpu.VMEM((IMG_H + 2 * HALF, IMG_W + 2 * EDGE, width), F32)
    conv, normed = pl.pallas_call(
        front_body,
        out_shape=(
            jax.ShapeDtypeStruct((tokens, width), F32),
            jax.ShapeDtypeStruct((tokens, width), BF),
        ),
        in_specs=[vmem] * 5,
        out_specs=(vmem, vmem),
        scratch_shapes=[pad],
        compiler_params=pltpu.CompilerParams(vmem_limit_bytes=24 << 20),
    )(patches, conv_weight, bias, gain, shift)

    flat = expert_ids.reshape(-1)
    table = (flat[:, None] == jnp.arange(n_exp, dtype=jnp.int32)[None, :]).astype(BF)
    pairs = TOP * tokens
    before = jnp.tril(jnp.ones((pairs, pairs), BF), -1)
    earlier = jnp.dot(before, table, preferred_element_type=F32)
    slots = jnp.sum(earlier * table.astype(F32), axis=1).astype(jnp.int32)
    positions = (flat * cap + slots).reshape(tokens, TOP)
    meta = jnp.concatenate(
        [positions.astype(F32).T, gate_weights.T, jnp.zeros((8 - 2 * TOP, tokens), F32)], axis=0
    )

    dma = pltpu.SemaphoreType.DMA
    chips = n_exp // 2
    mixed, grad_normed, gw_in, gw_out = pl.pallas_call(
        functools.partial(moe_body, n_dp, n_exp, cap),
        out_shape=(
            jax.ShapeDtypeStruct((tokens, width), BF),
            jax.ShapeDtypeStruct((tokens, width), F32),
            jax.ShapeDtypeStruct((depth, hid), F32),
            jax.ShapeDtypeStruct((depth, hid), F32),
        ),
        in_specs=[vmem] * 8,
        out_specs=(vmem,) * 4,
        scratch_shapes=[
            pltpu.VMEM((width, hid), BF),
            pltpu.VMEM((width, hid), BF),
            pltpu.VMEM((n_exp, tokens, width), BF),
            pltpu.VMEM((n_exp, tokens, width), BF),
            pltpu.VMEM((n_exp, 8, tokens), F32),
            pltpu.VMEM((count, width), BF),
            pltpu.VMEM((count, width), BF),
            pltpu.VMEM((count, hid), F32),
            pltpu.VMEM((count, hid), BF),
            pltpu.VMEM((count, hid), BF),
            pltpu.VMEM((count, width), BF),
            pltpu.VMEM((count, width), BF),
            pltpu.VMEM((count, width), BF),
            pltpu.VMEM((count, width), BF),
            pltpu.VMEM((n_dp, depth, hid), BF),
            pltpu.VMEM((n_dp, depth, hid), BF),
            pltpu.VMEM((n_dp, depth, hid), BF),
            pltpu.VMEM((n_dp, depth, hid), BF),
            dma((2, n_dp)),
            dma((2, n_dp)),
            dma((n_exp,)),
            dma((n_exp,)),
            dma((2, 2, chips)),
            dma((2, 2, chips)),
            dma((2, 2, chips)),
            dma((2, 2, chips)),
            dma((2, n_exp)),
            dma((2, n_exp)),
            dma((2, n_dp)),
            dma((2, n_dp)),
        ],
        compiler_params=pltpu.CompilerParams(
            collective_id=0, has_side_effects=True, vmem_limit_bytes=56 << 20
        ),
    )(normed, grad_mixed, meta, positions, gate_weights, patches, w_in[0], w_out[0])

    grad_input = pl.pallas_call(
        back_body,
        out_shape=jax.ShapeDtypeStruct((tokens, width), F32),
        in_specs=[vmem] * 5,
        out_specs=vmem,
        scratch_shapes=[pad],
        compiler_params=pltpu.CompilerParams(vmem_limit_bytes=24 << 20),
    )(conv, conv_weight, gain, grad_normed, grad_mixed)
    return mixed, grad_input, gw_in[None], gw_out[None]


def solution(mesh):
    rows = P(("dp", "expert"), None)
    split = P("expert", "dp", None)
    return jax.shard_map(
        local,
        mesh=mesh,
        in_specs=(rows, rows, rows, P(), P(), P(), P(), split, split, rows),
        out_specs=(rows, rows, split, split),
        check_vma=False,
    )
```

time: 199 us -> 132 us (0.66)
  Pallas kernels: 0 us -> 122 us
  waiting for transfers between devices: 94.3 us -> 0 us
  other arithmetic: 28 us -> 1.31 us
  matrix products: 24.6 us -> 0.26 us
  starting transfers between devices: 17.7 us -> 0 us
  between operations: 14.6 us -> 0.75 us
  local copies, waits for them, and re-layouts: 19.3 us -> 7.63 us
    pallas_call x0 -> x3, Pallas kernels: none -> 122 us  [the longest x1 111 us: local(): pl.pallas_call(functools.partial(moe_body, n_dp, n_exp, cap), out_shape=(...]
    all_to_all x4 -> x0, waiting for transfers between devices: 92.9 us -> none  [the longest x1 24.3 us: local(): lax.all_to_all(sent, 'expert', split_axis=0, concat_axis=0, tiled=True)]
    dot_general x8 -> x1, matrix products: 24.6 us -> 0.26 us  [local(): earlier = jnp.dot(before, table, preferred_element_type=F32)]
    all_to_all x4 -> x0, starting transfers between devices: 17.4 us -> none  [the longest x1 6.33 us: local(): lax.all_to_all(sent, 'expert', split_axis=0, concat_axis=0, tiled=True)]
    reduce_sum x8 -> x0, other arithmetic: 8.62 us -> none  [the longest x1 4.99 us: front(): mean = jnp.mean(total, axis=-1, keepdims=True)]
    add_any x2 -> x0, other arithmetic: 6.13 us -> none  [front(): padded[:, row:row + IMG_H, col:col + IMG_W, :]]
    slice x4 -> x0, local copies, waits for them, and re-layouts: 3.95 us -> none  [the longest x3 3.74 us: front(): conv_weight[row * KSIZE + col]]
    mul x4 -> x1, other arithmetic: 3.52 us -> 0.01 us  [local(): positions = (flat * cap + slots).reshape(tokens, TOP)]
  transfers between devices with their start and end apart: 7 -> 0, of which waited for: 4 -> 0; matrix products, arithmetic and copies ran while one was open for 27% -> 0% of each run, Pallas kernels for 0% -> 0%
where the time goes in v1:
time: 132 us
  Pallas kernels  122 us (92%)
  local copies, waits for them, and re-layouts  7.63 us (6%)
    pallas_call x1, Pallas kernels, local(): pl.pallas_call(functools.partial(moe_body, n_dp, n_exp, cap), out_shape=(...  111 us
    unnamed x31, local copies, waits for them, and re-layouts  7.11 us
    pallas_call x1, Pallas kernels, local(): pl.pallas_call(back_body, out_shape=jax.ShapeDtypeStruct((tokens, width),...  5.92 us
    pallas_call x1, Pallas kernels, local(): pl.pallas_call(front_body, out_shape=(jax.ShapeDtypeStruct((tokens, width...  5.07 us

profile of v1, /device:TPU:0, one launch (start us, length us, event | category | flops | bytes accessed | tf_op | source)
XLA Modules:
  0.0 131.6 jit_solution(10595509723397649920)
XLA Ops:
  0.6 0.0 copy-start.11
  0.7 0.1 pad.2.clone
  0.7 0.6 copy-done.11
  1.3 0.1 copy.24
  1.4 0.1 copy.23
  1.6 0.1 eq.15
  1.7 0.0 copy-start.2
  1.7 0.3 fusion
  2.0 0.0 copy-start
  2.0 0.1 convert_element_type.19
  2.1 0.6 convert_bitcast_fusion
  2.8 0.0 copy-start.12
  2.8 0.1 copy.25
  2.8 0.6 copy-done.12
  3.5 0.7 maximum_maximum_fusion.meta_ref
  4.1 0.0 copy-start.5
  4.1 0.0 copy-start.6
  4.1 0.0 copy-start.7
  4.1 0.7 copy.26.gate_ref
  4.9 0.0 copy-done.2
  4.9 0.0 copy-done
  4.9 0.0 copy-done.5
  4.9 0.0 copy-done.6
  4.9 0.0 copy-done.7
  4.9 5.1 %shard_map.129 = (f32[128,1024]{1,0:T(8,128)S(1)}, bf16[128,1024]{1,0:T(8,128)(2,1)S(1)}) custom-call(bf16[128,1024]{1,0:T(8,128)(2,1)S(1)} %copy-done, f32[49,1024]{1,0:T(8,128)S(1)} %copy-done.2, f32[1,1024]{1,0:T(1,128)S(1)} %bitcast.12, f32[1,1024]{1,0:T(1,128)S(1)} %bitcast.10, f32[1,1024]{1,0:T(1,128)S(1)} %bitcast.13), custom_call_target="tpu_custom_call" | custom-call | tf_op jit(solution)/shard_map/pallas_call | solution.py:435
  10.0 0.0 copy-start.4
  10.0 0.7 copy-done.4
  10.7 0.0 copy-start.1
  10.7 110.6 %shard_map.130 = (bf16[128,1024]{1,0:T(8,128)(2,1)}, f32[128,1024]{1,0:T(8,128)}, f32[256,1024]{1,0:T(8,128)}, f32[256,1024]{1,0:T(8,128)}) custom-call(bf16[128,1024]{1,0:T(8,128)(2,1)} %copy-done.4, bf16[128,1024]{1,0:T(8,128)(2,1)} %cot_ref.3, f32[8,128]{1,0:T(8,128)} %maximum_maximum_fusion.meta_ref, s32[128,2]{1,0:T(8,128)} %get-tuple-element.17.pos_ref, ...), custom_call_target="tpu_custom_call" | custom-call | tf_op jit(solution)/shard_map/pallas_call | solution.py:460
  121.3 0.0 copy-done.1
  121.3 0.0 copy-start.3
  121.3 1.0 copy-done.3
  122.4 0.0 copy-start.10
  122.4 0.0 copy-start.9
  122.4 5.9 %shard_map.131 = f32[128,1024]{1,0:T(8,128)} custom-call(f32[128,1024]{1,0:T(8,128)S(1)} %get-tuple-element.12.conv_ref, f32[49,1024]{1,0:T(8,128)S(1)} %copy-done.2, f32[1,1024]{1,0:T(1,128)S(1)} %bitcast.11, f32[128,1024]{1,0:T(8,128)S(1)} %copy-done.3, bf16[128,1024]{1,0:T(8,128)(2,1)S(1)} %copy-done.1), custom_call_target="tpu_custom_call" | custom-call | tf_op jit(solution)/shard_map/pallas_call | solution.py:507
  128.3 0.0 copy-done.10
  128.3 0.7 copy.30
  129.0 0.0 copy-done.9
  129.0 0.0 copy-start.8
  129.0 1.0 copy.31
  130.0 0.6 copy-done.8
  130.6 1.0 copy.32
  (4 shorter events, 0.0 us)
Async XLA Ops:
  0.6 0.7 copy-start.11
  1.7 3.2 %copy-start.2 = (f32[49,1024]{1,0:T(8,128)S(1)}, f32[49,1024]{1,0:T(8,128)}, u32[]{:S(2)}) copy-start(f32[49,1024]{1,0:T(8,128)} %weight_ref.3) | copy-start | bytes 602116
  2.0 2.9 %copy-start = (bf16[128,1024]{1,0:T(8,128)(2,1)S(1)}, bf16[128,1024]{1,0:T(8,128)(2,1)}, u32[]{:S(2)}) copy-start(bf16[128,1024]{1,0:T(8,128)(2,1)} %patches_ref.3) | copy-start | bytes 786436
  2.8 0.7 copy-start.12
  4.1 0.8 copy-start.5
  4.1 0.8 copy-start.6
  4.1 0.8 copy-start.7
  10.0 0.7 copy-start.4
  10.7 110.6 %copy-start.1 = (bf16[128,1024]{1,0:T(8,128)(2,1)S(1)}, bf16[128,1024]{1,0:T(8,128)(2,1)}, u32[]{:S(2)}) copy-start(bf16[128,1024]{1,0:T(8,128)(2,1)} %cot_ref.3) | copy-start | bytes 786436
  121.3 1.0 copy-start.3
  122.4 5.9 %copy-start.10 = (bf16[128,1024]{1,0:T(8,128)(2,1)S(1)}, bf16[128,1024]{1,0:T(8,128)(2,1)}, u32[]{:S(2)}) copy-start(bf16[128,1024]{1,0:T(8,128)(2,1)} %get-tuple-element.22) | copy-start | bytes 786436
  122.4 6.6 %copy-start.9 = (f32[256,1024]{1,0:T(8,128)S(1)}, f32[256,1024]{1,0:T(8,128)}, u32[]{:S(2)}) copy-start(f32[256,1024]{1,0:T(8,128)} %get-tuple-element.14) | copy-start | bytes 3145732
  129.0 1.6 %copy-start.8 = (f32[256,1024]{1,0:T(8,128)S(1)}, f32[256,1024]{1,0:T(8,128)}, u32[]{:S(2)}) copy-start(f32[256,1024]{1,0:T(8,128)} %get-tuple-element.15) | copy-start | bytes 3145732

commit v2 on v1

v2 whole, which is shorter than its diff:
```python
import functools

import jax
import jax.numpy as jnp
from jax import lax
from jax.experimental import pallas as pl
from jax.experimental.pallas import tpu as pltpu
from jax.sharding import PartitionSpec as P

KSIZE = 7
HALF = KSIZE // 2
TOP = 2
IMG_W = 16
IMG_H = 8
EPS = 1e-06
EDGE = 8
MESH = pl.DeviceIdType.MESH
BF = jnp.bfloat16
F32 = jnp.float32


def conv_into(pad, weight_ref, out_ref, bias_ref, flip):
    width = out_ref.shape[1]

    def chunk(i, carry):
        lanes = pl.ds(pl.multiple_of(i * 128, 128), 128)
        total = jnp.zeros((IMG_H, IMG_W, 128), F32)
        if bias_ref is not None:
            total = total + bias_ref[0:1, lanes].reshape(1, 1, 128)
        for col in range(KSIZE):
            start = EDGE - HALF + col
            slab = pad[:, start : start + IMG_W, lanes]
            for row in range(KSIZE):
                tap = row * KSIZE + col
                if flip:
                    tap = KSIZE * KSIZE - 1 - tap
                total = total + slab[row : row + IMG_H] * weight_ref[tap : tap + 1, lanes].reshape(
                    1, 1, 128
                )
        out_ref[:, lanes] = total.reshape(IMG_H * IMG_W, 128)
        return carry

    lax.fori_loop(0, width // 128, chunk, 0)


def fill_pad(pad, image):
    pad[...] = jnp.zeros_like(pad)
    pad[HALF : HALF + IMG_H, EDGE : EDGE + IMG_W, :] = image.reshape(IMG_H, IMG_W, image.shape[-1])


def normalise(conv):
    centred = conv - jnp.mean(conv, axis=1, keepdims=True)
    spread = jnp.mean(centred * centred, axis=1, keepdims=True)
    scale = lax.rsqrt(spread + EPS)
    return centred * scale, scale


def dot(left, right, dims):
    return lax.dot_general(left, right, (dims, ((), ())), preferred_element_type=F32)


NN = ((1,), (0,))
NT = ((1,), (1,))
TN = ((0,), (0,))


def moe_body(
    n_dp,
    n_exp,
    cap,
    patches_ref,
    ids_ref,
    gate_ref,
    taps_ref,
    bias_ref,
    gain_ref,
    shift_ref,
    w_in_ref,
    w_out_ref,
    cot_ref,
    mixed_ref,
    grad_ref,
    gw_in_ref,
    gw_out_ref,
    pad,
    conv,
    normed,
    meta,
    flip,
    win,
    wout,
    all_n,
    all_c,
    all_m,
    rows,
    grads,
    slope,
    hidden,
    ghid,
    outs,
    back,
    r_outs,
    r_back,
    part_in,
    part_out,
    first_got,
    staged,
    second_got,
    w_send,
    w_recv,
    m_send,
    m_recv,
    line_send,
    line_recv,
    twin_send,
    twin_recv,
    ret_send,
    ret_recv,
    g_send,
    g_recv,
    h_send,
    h_recv,
):
    dp = lax.axis_index("dp")
    ex = lax.axis_index("expert")
    chips = n_exp // 2
    chip = ex // 2
    core = ex % 2
    depth, hid = w_in_ref.shape
    tokens, width = patches_ref.shape
    count = n_exp * cap
    tile = 256
    sides = grid_of(n_dp)
    spot = (dp // sides[1], dp % sides[1])
    half = depth // 2

    def dp_at(first, second, turned):
        return second * sides[1] + first if turned else first * sides[1] + second

    barrier = pltpu.get_barrier_semaphore()
    for i in range(1, n_exp):
        pl.semaphore_signal(
            barrier, inc=1, device_id=(dp, (ex + i) % n_exp), device_id_type=MESH
        )
    for i in range(1, n_dp):
        pl.semaphore_signal(barrier, inc=1, device_id=((dp + i) % n_dp, ex), device_id_type=MESH)
    pl.semaphore_wait(barrier, n_exp - 1 + n_dp - 1)

    def remote(src, dst, send, recv, to):
        return pltpu.make_async_remote_copy(
            src_ref=src, dst_ref=dst, send_sem=send, recv_sem=recv, device_id=to, device_id_type=MESH
        )

    full = (win, wout)
    shard = (w_in_ref, w_out_ref)
    started = []

    def sides_of(h):
        return sides[1 - h], spot[1 - h], sides[h], spot[h]

    def half_at(who, h):
        return pl.ds(pl.multiple_of(who * depth + h * half, 16), half)

    def weight_copy(a, h, i, j, own):
        n_one, one, n_two, two = sides_of(h)
        origin = dp_at((one - i) % n_one, two, h == 0)
        if j == 0:
            to = dp_at((one + i) % n_one, two, h == 0)
            origin = dp
        else:
            to = dp_at(one, (two + j) % n_two, h == 0)
        src = shard[a].at[pl.ds(h * half, half)] if own else full[a].at[half_at(origin, h)]
        return remote(
            src,
            full[a].at[half_at(origin, h)],
            w_send.at[a, h, i, j],
            w_recv.at[a, h, i, j],
            (to, ex),
        )

    def weights_first(a):
        for h in range(2):
            n_one, _, n_two, _ = sides_of(h)
            for i in range(1, n_one):
                copy = weight_copy(a, h, i, 0, True)
                copy.start()
                started.append(copy)
        for h in range(2):
            n_one, _, n_two, _ = sides_of(h)
            for j in range(1, n_two):
                copy = weight_copy(a, h, 0, j, True)
                copy.start()
                started.append(copy)

    def weights_on(a):
        for h in range(2):
            n_one, _, n_two, _ = sides_of(h)
            for i in range(1, n_one):
                weight_copy(a, h, i, 0, True).wait_recv()
                for j in range(1, n_two):
                    copy = weight_copy(a, h, i, j, False)
                    copy.start()
                    started.append(copy)

    def weights_done(a):
        for h in range(2):
            n_one, _, n_two, _ = sides_of(h)
            for i in range(n_one):
                for j in range(1, n_two):
                    weight_copy(a, h, i, j, i == 0).wait_recv()

    own = (normed, cot_ref)
    held = (all_n, all_c)

    def line(a, way, k, src_dev, src):
        step = 1 if way == 0 else -1
        return remote(
            src,
            held[a].at[src_dev],
            line_send.at[a, way, k],
            line_recv.at[a, way, k],
            (dp, jnp.clip(ex + 2 * step, core, n_exp - 2 + core)),
        )

    def twin(a, way, k, src_dev, src):
        return remote(
            src,
            held[a].at[src_dev],
            twin_send.at[a, way, k],
            twin_recv.at[a, way, k],
            (dp, 2 * chip + 1 - core),
        )

    def each(way, k):
        if way == 0:
            return chip - k >= 0, chip + 1 < chips, ex - 2 * k
        return chip + k < chips, chip - 1 >= 0, ex + 2 * k

    def send_step(a, k):
        for way in range(2):
            there, ahead, src_dev = each(way, k)
            src_dev = jnp.clip(src_dev, 0, n_exp - 1)
            src = own[a] if k == 0 else held[a].at[src_dev]
            if k > 0:

                @pl.when(there)
                def _(a=a, way=way, k=k, src_dev=src_dev, src=src):
                    line(a, way, k - 1, src_dev, src).wait_recv()

            if k < chips - 1:

                @pl.when(jnp.logical_and(there, ahead))
                def _(a=a, way=way, k=k, src_dev=src_dev, src=src):
                    line(a, way, k, src_dev, src).start()

            if k > 0:

                @pl.when(there)
                def _(a=a, way=way, k=k, src_dev=src_dev, src=src):
                    twin(a, way, k, src_dev, src).start()

            elif way == 1:
                twin(a, 0, k, src_dev, src).start()

    def finish_twins(a):
        for k in range(chips):
            for way in range(2):
                if k == 0 and way == 1:
                    continue
                there, _, src_dev = each(way, k)
                other = jnp.clip(src_dev + 1 - 2 * core, 0, n_exp - 1)

                @pl.when(there)
                def _(a=a, way=way, k=k, other=other):
                    twin(a, way, k, other, held[a].at[other]).wait_recv()

    def finish_sends(a):
        for k in range(chips):
            for way in range(2):
                there, ahead, src_dev = each(way, k)
                src_dev = jnp.clip(src_dev, 0, n_exp - 1)
                if k < chips - 1:

                    @pl.when(jnp.logical_and(there, ahead))
                    def _(a=a, way=way, k=k, src_dev=src_dev):
                        line(a, way, k, src_dev, own[a]).wait_send()

                if k > 0 or way == 0:

                    @pl.when(there)
                    def _(a=a, way=way, k=k, src_dev=src_dev):
                        twin(a, way, k, src_dev, own[a]).wait_send()

    send_step(1, 0)
    weights_first(0)
    weights_first(1)

    fill_pad(pad, patches_ref[...].astype(F32))
    conv_into(pad, taps_ref, conv, bias_ref, False)
    unit, _ = normalise(conv[...])
    normed[...] = (unit * gain_ref[...] + shift_ref[...]).astype(BF)
    send_step(0, 0)

    flip[...] = jnp.zeros_like(flip)
    flip[:, 0:TOP] = ids_ref[...].astype(F32)
    flip[:, TOP : 2 * TOP] = gate_ref[...]
    turned = jnp.transpose(flip[...])
    names = lax.broadcasted_iota(jnp.int32, (n_exp, tokens), 0).astype(F32)
    named = [jnp.where(names == turned[k : k + 1, :], 1.0, 0.0) for k in range(TOP)]
    before = lax.broadcasted_iota(jnp.int32, (tokens, tokens), 0) < lax.broadcasted_iota(
        jnp.int32, (tokens, tokens), 1
    )
    table = named[0]
    for k in range(1, TOP):
        table = table + named[k]
    rank = dot(table.astype(BF), jnp.where(before, 1.0, 0.0).astype(BF), NN)
    places = [
        turned[k : k + 1, :] * cap + jnp.sum(named[k] * rank, axis=0, keepdims=True)
        for k in range(TOP)
    ]
    meta[...] = jnp.zeros_like(meta)
    for k in range(TOP):
        meta[k : k + 1, :] = places[k]
        meta[TOP + k : TOP + k + 1, :] = turned[TOP + k : TOP + k + 1, :]
    metas = []
    for i in range(1, n_exp):
        copy = remote(meta, all_m.at[ex], m_send.at[i], m_recv.at[i], (dp, (ex + i) % n_exp))
        copy.start()
        metas.append(copy)

    mine = pl.ds(pl.multiple_of(dp * depth, 16), depth)
    win[mine] = w_in_ref[...]
    wout[mine] = w_out_ref[...]
    all_n[ex] = normed[...]
    all_c[ex] = cot_ref[...]
    all_m[ex] = meta[...]
    for k in range(1, max(chips, 2)):
        if k < chips:
            send_step(1, k)
        if k == 1:
            weights_on(0)
        if k < chips:
            send_step(0, k)
        if k == 1:
            weights_on(1)
    for copy in metas:
        copy.wait()

    slots = lax.broadcasted_iota(jnp.int32, (cap, tokens), 0).astype(F32) + (ex * cap).astype(F32)

    def choose(j):
        info = all_m[j]
        hits = [jnp.where(slots == info[k : k + 1, :], 1.0, 0.0) for k in range(TOP)]
        weighed = hits[0] * info[TOP : TOP + 1, :]
        for k in range(1, TOP):
            weighed = weighed + hits[k] * info[TOP + k : TOP + k + 1, :]
        select = hits[0]
        for k in range(1, TOP):
            select = select + hits[k]
        return select.astype(BF), jnp.sum(weighed, axis=1, keepdims=True)

    finish_twins(1)

    def gather_grads(j, carry):
        select, gate = choose(j)
        at = pl.ds(pl.multiple_of(j * cap, 16), cap)
        grads[at] = (dot(select, all_c[j], NN) * gate).astype(BF)
        return carry

    lax.fori_loop(0, n_exp, gather_grads, 0)
    finish_twins(0)

    def gather_rows(j, carry):
        select, _ = choose(j)
        at = pl.ds(pl.multiple_of(j * cap, 16), cap)
        rows[at] = dot(select, all_n[j], NN).astype(BF)
        return carry

    lax.fori_loop(0, n_exp, gather_rows, 0)
    weights_done(0)

    def up(n, carry):
        cols = pl.ds(pl.multiple_of(n * tile, tile), tile)
        x = dot(rows[...], win[:, cols], NN)
        c = 0.7978845608028654
        t = jnp.tanh(c * (x + 0.044715 * (x * x * x)))
        side = 0.5 * (1.0 + t)
        hidden[:, cols] = (x * side).astype(BF)
        slope[:, cols] = side + 0.5 * x * (1.0 - t * t) * (c * (1.0 + 3 * 0.044715 * (x * x)))
        return carry

    lax.fori_loop(0, hid // tile, up, 0)

    parts = (part_in, part_out)
    shares = []

    def first_share(a, h, j, i):
        n_one, one, n_two, two = sides_of(h)
        whose = dp_at(i, (two + j) % n_two, h == 0)
        to = dp_at(one, (two + j) % n_two, h == 0)
        return remote(
            parts[a].at[whose, pl.ds(h * half, half)],
            first_got.at[a, h, j - 1, i],
            g_send.at[a, h, j, i],
            g_recv.at[a, h, j, i],
            (to, ex),
        )

    def weight_grad(a, left, right):
        part = parts[a]
        if depth % 128 == 0:
            for i in range(1, n_dp + 1):
                to = (dp + i) % n_dp
                cols = pl.ds(pl.multiple_of(to * depth, depth), depth)
                part[to] = dot(left[:, cols], right[...], TN).astype(BF)
        else:

            def some(n, carry):
                cols = pl.ds(pl.multiple_of(n * tile, tile), tile)
                made = dot(left[:, cols], right[...], TN).astype(BF)
                many = tile // depth
                part[pl.ds(n * many, many)] = made.reshape(many, depth, hid)
                return carry

            lax.fori_loop(0, width // tile, some, 0)
        for h in range(2):
            n_one, _, n_two, _ = sides_of(h)
            for j in range(1, n_two):
                for i in range(n_one):
                    copy = first_share(a, h, j, i)
                    copy.start()
                    shares.append(copy)

    def met(a, h, place):
        n_one, one, n_two, two = sides_of(h)
        value = parts[a][dp_at(place, two, h == 0), pl.ds(h * half, half)].astype(F32)
        for j in range(1, n_two):
            value = value + first_got[a, h, j - 1, place].astype(F32)
        return value

    def second_shares(a):
        for h in range(2):
            n_one, one, n_two, two = sides_of(h)
            for j in range(1, n_two):
                for i in range(n_one):
                    first_share(a, h, j, i).wait_recv()
            for i in range(1, n_one):
                place = (one + i) % n_one
                staged[a, h, i - 1] = met(a, h, place).astype(BF)
                copy = remote(
                    staged.at[a, h, i - 1],
                    second_got.at[a, h, i - 1],
                    h_send.at[a, h, i],
                    h_recv.at[a, h, i],
                    (dp_at(place, two, h == 0), ex),
                )
                copy.start()
                seconds[a].append(copy)

    seconds = ([], [])

    def weight_sum(a, out):
        for copy in seconds[a]:
            copy.wait()
        for h in range(2):
            n_one, one, n_two, two = sides_of(h)
            value = met(a, h, one)
            for i in range(1, n_one):
                value = value + second_got[a, h, i - 1].astype(F32)
            out[pl.ds(h * half, half)] = value

    weights_done(1)

    def down(n, carry):
        cols = pl.ds(pl.multiple_of(n * tile, tile), tile)
        outs[:, cols] = dot(hidden[...], wout[cols, :], NT).astype(BF)
        return carry

    lax.fori_loop(0, width // tile, down, 0)

    my_rows = pl.ds(pl.multiple_of(ex * cap, 16), cap)

    def give_back(a, src, dst):
        copies = []
        for i in range(1, n_exp):
            to = (ex + i) % n_exp
            copy = remote(
                src.at[pl.ds(pl.multiple_of(to * cap, 16), cap)],
                dst.at[my_rows],
                ret_send.at[a, i],
                ret_recv.at[a, i],
                (dp, to),
            )
            copy.start()
            copies.append(copy)
        dst[my_rows] = src[my_rows]
        return copies

    outs_back = give_back(0, outs, r_outs)
    weight_grad(1, grads, hidden)

    def down_grad(n, carry):
        cols = pl.ds(pl.multiple_of(n * tile, tile), tile)
        ghid[:, cols] = (dot(grads[...], wout[:, cols], NN) * slope[:, cols]).astype(BF)
        return carry

    lax.fori_loop(0, hid // tile, down_grad, 0)

    def up_grad(n, carry):
        cols = pl.ds(pl.multiple_of(n * tile, tile), tile)
        back[:, cols] = dot(ghid[...], win[cols, :], NT).astype(BF)
        return carry

    lax.fori_loop(0, width // tile, up_grad, 0)
    grads_back = give_back(1, back, r_back)
    weight_grad(0, rows, ghid)
    second_shares(1)

    tall = lax.broadcasted_iota(jnp.int32, (count, tokens), 0).astype(F32)
    ones = [jnp.where(tall == meta[k : k + 1, :], 1.0, 0.0).astype(BF) for k in range(TOP)]
    for copy in outs_back:
        copy.wait()
    combined = dot(ones[0], r_outs[...], TN) * gate_ref[:, 0:1]
    for k in range(1, TOP):
        combined = combined + dot(ones[k], r_outs[...], TN) * gate_ref[:, k : k + 1]
    mixed_ref[...] = (patches_ref[...].astype(F32) + combined).astype(BF)
    second_shares(0)

    for copy in grads_back:
        copy.wait()
    both = ones[0]
    for k in range(1, TOP):
        both = both + ones[k]
    unit, scale = normalise(conv[...])
    lean = dot(both, r_back[...], TN) * gain_ref[...]
    inner = lean - jnp.mean(lean, axis=1, keepdims=True)
    inner = inner - unit * jnp.mean(lean * unit, axis=1, keepdims=True)
    fill_pad(pad, inner * scale)
    conv_into(pad, taps_ref, grad_ref, None, True)
    grad_ref[...] += cot_ref[...].astype(F32)

    weight_sum(1, gw_out_ref)
    weight_sum(0, gw_in_ref)
    for copy in started + shares:
        copy.wait_send()
    finish_sends(0)
    finish_sends(1)


def grid_of(n_dp):
    side = max(i for i in range(1, n_dp + 1) if n_dp % i == 0 and i * i <= n_dp)
    return side, n_dp // side


def local(
    patches,
    expert_ids,
    gate_weights,
    conv_weight,
    conv_bias,
    ln_gain,
    ln_shift,
    w_in,
    w_out,
    grad_mixed,
):
    tokens, width = patches.shape
    depth, hid = w_in.shape[1:]
    n_exp = lax.axis_size("expert")
    n_dp = lax.axis_size("dp")
    cap = 4 * tokens // n_exp
    count = n_exp * cap
    vmem = pl.BlockSpec(memory_space=pltpu.VMEM)
    dma = pltpu.SemaphoreType.DMA
    chips = n_exp // 2
    long = max(grid_of(n_dp))
    more = max(long - 1, 1)
    half = depth // 2
    mixed, grad_input, gw_in, gw_out = pl.pallas_call(
        functools.partial(moe_body, n_dp, n_exp, cap),
        out_shape=(
            jax.ShapeDtypeStruct((tokens, width), BF),
            jax.ShapeDtypeStruct((tokens, width), F32),
            jax.ShapeDtypeStruct((depth, hid), F32),
            jax.ShapeDtypeStruct((depth, hid), F32),
        ),
        in_specs=[vmem] * 10,
        out_specs=(vmem,) * 4,
        scratch_shapes=[
            pltpu.VMEM((IMG_H + 2 * HALF, IMG_W + 2 * EDGE, width), F32),
            pltpu.VMEM((tokens, width), F32),
            pltpu.VMEM((tokens, width), BF),
            pltpu.VMEM((8, tokens), F32),
            pltpu.VMEM((tokens, 128), F32),
            pltpu.VMEM((width, hid), BF),
            pltpu.VMEM((width, hid), BF),
            pltpu.VMEM((n_exp, tokens, width), BF),
            pltpu.VMEM((n_exp, tokens, width), BF),
            pltpu.VMEM((n_exp, 8, tokens), F32),
            pltpu.VMEM((count, width), BF),
            pltpu.VMEM((count, width), BF),
            pltpu.VMEM((count, hid), F32),
            pltpu.VMEM((count, hid), BF),
            pltpu.VMEM((count, hid), BF),
            pltpu.VMEM((count, width), BF),
            pltpu.VMEM((count, width), BF),
            pltpu.VMEM((count, width), BF),
            pltpu.VMEM((count, width), BF),
            pltpu.VMEM((n_dp, depth, hid), BF),
            pltpu.VMEM((n_dp, depth, hid), BF),
            pltpu.VMEM((2, 2, more, long, half, hid), BF),
            pltpu.VMEM((2, 2, more, half, hid), BF),
            pltpu.VMEM((2, 2, more, half, hid), BF),
            dma((2, 2, long, long)),
            dma((2, 2, long, long)),
            dma((n_exp,)),
            dma((n_exp,)),
            dma((2, 2, chips)),
            dma((2, 2, chips)),
            dma((2, 2, chips)),
            dma((2, 2, chips)),
            dma((2, n_exp)),
            dma((2, n_exp)),
            dma((2, 2, long, long)),
            dma((2, 2, long, long)),
            dma((2, 2, long)),
            dma((2, 2, long)),
        ],
        compiler_params=pltpu.CompilerParams(
            collective_id=0, has_side_effects=True, vmem_limit_bytes=58 << 20
        ),
    )(
        patches,
        expert_ids,
        gate_weights,
        conv_weight,
        conv_bias[None],
        ln_gain[None],
        ln_shift[None],
        w_in[0],
        w_out[0],
        grad_mixed,
    )
    return mixed, grad_input, gw_in[None], gw_out[None]


def solution(mesh):
    rows = P(("dp", "expert"), None)
    split = P("expert", "dp", None)
    return jax.shard_map(
        local,
        mesh=mesh,
        in_specs=(rows, rows, rows, P(), P(), P(), P(), split, split, rows),
        out_specs=(rows, rows, split, split),
        check_vma=False,
    )
```

time: 132 us -> 107 us (0.81)
  the two profiles are of different devices: /device:TPU:0 before, /device:TPU:9 now
where the time goes in v2:
time: 107 us; the launch traced here: 106 us
  Pallas kernels  97.3 us (91%)
  local copies, waits for them, and re-layouts  8.37 us (8%)
    pallas_call x1, Pallas kernels, local(): pl.pallas_call(functools.partial(moe_body, n_dp, n_exp, cap), out_shape=(...  97.3 us
    unnamed x14, local copies, waits for them, and re-layouts  8.37 us

profile of v2, /device:TPU:9, one launch (start us, length us, event | category | flops | bytes accessed | tf_op | source)
XLA Modules:
  0.0 106.4 jit_solution(18283873655355791163)
XLA Ops:
  0.6 0.0 copy-start.2
  0.6 0.7 copy-done.2
  1.3 0.0 copy-start.3
  1.3 0.7 copy.14.ids_ref
  2.1 0.0 copy-done.3
  2.1 0.7 copy.15.gate_ref
  2.8 97.3 %shard_map.129 = (bf16[128,1024]{1,0:T(8,128)(2,1)}, f32[128,1024]{1,0:T(8,128)}, f32[256,1024]{1,0:T(8,128)}, f32[256,1024]{1,0:T(8,128)}) custom-call(bf16[128,1024]{1,0:T(8,128)(2,1)} %patches_ref.1, s32[128,2]{1,0:T(8,128)} %copy.14.ids_ref, f32[128,2]{1,0:T(8,128)} %copy.15.gate_ref, f32[49,1024]{1,0:T(8,128)} %taps_ref.1, f32[1,1024]{1,0:T(1,128)} %bitcast.11, ...), custom_call_target="tpu_custom_call" | custom-call | tf_op jit(solution)/shard_map/pallas_call | solution.py:579
  100.1 0.0 copy-start.1
  100.1 1.8 %copy.20 = bf16[128,1024]{1,0:T(8,128)(2,1)} copy(bf16[128,1024]{1,0:T(8,128)(2,1)} %get-tuple-element.16) | data formatting | bytes 524288
  101.9 1.9 %copy.21 = f32[128,1024]{1,0:T(8,128)} copy(f32[128,1024]{1,0:T(8,128)} %get-tuple-element.17) | data formatting | bytes 1048576
  103.8 0.0 copy-done.1
  103.8 0.0 copy-start
  103.8 1.0 copy.22
  104.8 0.6 copy-done
  105.4 1.0 copy.23
Async XLA Ops:
  0.6 0.7 copy-start.2
  1.3 0.7 copy-start.3
  100.1 3.7 %copy-start.1 = (f32[256,1024]{1,0:T(8,128)S(1)}, f32[256,1024]{1,0:T(8,128)}, u32[]{:S(2)}) copy-start(f32[256,1024]{1,0:T(8,128)} %get-tuple-element.10) | copy-start | bytes 3145732
  103.8 1.6 %copy-start = (f32[256,1024]{1,0:T(8,128)S(1)}, f32[256,1024]{1,0:T(8,128)}, u32[]{:S(2)}) copy-start(f32[256,1024]{1,0:T(8,128)} %get-tuple-element.11) | copy-start | bytes 3145732

commit v3 on v2

--- a/solution.py
+++ b/solution.py
@@ -85,13 +85,13 @@
     pad,
     conv,
     normed,
-    meta,
     flip,
+    sent_n,
+    sent_g,
+    picked,
+    single,
     win,
     wout,
-    all_n,
-    all_c,
-    all_m,
     rows,
     grads,
     slope,
@@ -108,12 +108,6 @@
     second_got,
     w_send,
     w_recv,
-    m_send,
-    m_recv,
-    line_send,
-    line_recv,
-    twin_send,
-    twin_recv,
     ret_send,
     ret_recv,
     g_send,
@@ -123,9 +117,6 @@
 ):
     dp = lax.axis_index("dp")
     ex = lax.axis_index("expert")
-    chips = n_exp // 2
-    chip = ex // 2
-    core = ex % 2
     depth, hid = w_in_ref.shape
     tokens, width = patches_ref.shape
     count = n_exp * cap
@@ -144,7 +135,6 @@
         )
     for i in range(1, n_dp):
         pl.semaphore_signal(barrier, inc=1, device_id=((dp + i) % n_dp, ex), device_id_type=MESH)
-    pl.semaphore_wait(barrier, n_exp - 1 + n_dp - 1)
 
     def remote(src, dst, send, recv, to):
         return pltpu.make_async_remote_copy(
@@ -209,97 +199,23 @@
                 for j in range(1, n_two):
                     weight_copy(a, h, i, j, i == 0).wait_recv()
 
-    own = (normed, cot_ref)
-    held = (all_n, all_c)
-
-    def line(a, way, k, src_dev, src):
-        step = 1 if way == 0 else -1
-        return remote(
-            src,
-            held[a].at[src_dev],
-            line_send.at[a, way, k],
-            line_recv.at[a, way, k],
-            (dp, jnp.clip(ex + 2 * step, core, n_exp - 2 + core)),
-        )
-
-    def twin(a, way, k, src_dev, src):
-        return remote(
-            src,
-            held[a].at[src_dev],
-            twin_send.at[a, way, k],
-            twin_recv.at[a, way, k],
-            (dp, 2 * chip + 1 - core),
-        )
-
-    def each(way, k):
-        if way == 0:
-            return chip - k >= 0, chip + 1 < chips, ex - 2 * k
-        return chip + k < chips, chip - 1 >= 0, ex + 2 * k
-
-    def send_step(a, k):
-        for way in range(2):
-            there, ahead, src_dev = each(way, k)
-            src_dev = jnp.clip(src_dev, 0, n_exp - 1)
-            src = own[a] if k == 0 else held[a].at[src_dev]
-            if k > 0:
-
-                @pl.when(there)
-                def _(a=a, way=way, k=k, src_dev=src_dev, src=src):
-                    line(a, way, k - 1, src_dev, src).wait_recv()
-
-            if k < chips - 1:
-
-                @pl.when(jnp.logical_and(there, ahead))
-                def _(a=a, way=way, k=k, src_dev=src_dev, src=src):
-                    line(a, way, k, src_dev, src).start()
-
-            if k > 0:
-
-                @pl.when(there)
-                def _(a=a, way=way, k=k, src_dev=src_dev, src=src):
-                    twin(a, way, k, src_dev, src).start()
-
-            elif way == 1:
-                twin(a, 0, k, src_dev, src).start()
-
-    def finish_twins(a):
-        for k in range(chips):
-            for way in range(2):
-                if k == 0 and way == 1:
-                    continue
-                there, _, src_dev = each(way, k)
-                other = jnp.clip(src_dev + 1 - 2 * core, 0, n_exp - 1)
-
-                @pl.when(there)
-                def _(a=a, way=way, k=k, other=other):
-                    twin(a, way, k, other, held[a].at[other]).wait_recv()
-
-    def finish_sends(a):
-        for k in range(chips):
-            for way in range(2):
-                there, ahead, src_dev = each(way, k)
-                src_dev = jnp.clip(src_dev, 0, n_exp - 1)
-                if k < chips - 1:
-
-                    @pl.when(jnp.logical_and(there, ahead))
-                    def _(a=a, way=way, k=k, src_dev=src_dev):
-                        line(a, way, k, src_dev, own[a]).wait_send()
-
-                if k > 0 or way == 0:
-
-                    @pl.when(there)
-                    def _(a=a, way=way, k=k, src_dev=src_dev):
-                        twin(a, way, k, src_dev, own[a]).wait_send()
-
-    send_step(1, 0)
-    weights_first(0)
-    weights_first(1)
-
-    fill_pad(pad, patches_ref[...].astype(F32))
-    conv_into(pad, taps_ref, conv, bias_ref, False)
-    unit, _ = normalise(conv[...])
-    normed[...] = (unit * gain_ref[...] + shift_ref[...]).astype(BF)
-    send_step(0, 0)
+    my_rows = pl.ds(pl.multiple_of(ex * cap, 16), cap)
+
+    def exchange(a, src, dst):
+        copies = []
+        for i in range(1, n_exp):
+            to = (ex + i) % n_exp
+            copy = remote(
+                src.at[pl.ds(pl.multiple_of(to * cap, 16), cap)],
+                dst.at[my_rows],
+                ret_send.at[a, i],
+                ret_recv.at[a, i],
+                (dp, to),
+            )
+            copy.start()
+            copies.append(copy)
+        dst[my_rows] = src[my_rows]
+        return copies
 
     flip[...] = jnp.zeros_like(flip)
     flip[:, 0:TOP] = ids_ref[...].astype(F32)
@@ -318,65 +234,40 @@
         turned[k : k + 1, :] * cap + jnp.sum(named[k] * rank, axis=0, keepdims=True)
         for k in range(TOP)
     ]
-    meta[...] = jnp.zeros_like(meta)
+    tall = lax.broadcasted_iota(jnp.int32, (count, tokens), 0).astype(F32)
+    hits = [jnp.where(tall == places[k], 1.0, 0.0) for k in range(TOP)]
+    ones = [hit.astype(BF) for hit in hits]
+    weighed = hits[0] * turned[TOP : TOP + 1, :]
+    for k in range(1, TOP):
+        weighed = weighed + hits[k] * turned[TOP + k : TOP + k + 1, :]
+    gates = jnp.sum(weighed, axis=1, keepdims=True)
+    both_hits = hits[0]
+    for k in range(1, TOP):
+        both_hits = both_hits + hits[k]
+    picked[...] = both_hits.astype(BF)
     for k in range(TOP):
-        meta[k : k + 1, :] = places[k]
-        meta[TOP + k : TOP + k + 1, :] = turned[TOP + k : TOP + k + 1, :]
-    metas = []
-    for i in range(1, n_exp):
-        copy = remote(meta, all_m.at[ex], m_send.at[i], m_recv.at[i], (dp, (ex + i) % n_exp))
-        copy.start()
-        metas.append(copy)
+        single[k] = ones[k]
+
+    pl.semaphore_wait(barrier, n_exp - 1 + n_dp - 1)
+    weights_first(0)
+    sent_g[...] = (dot(picked[...], cot_ref[...], NN) * gates).astype(BF)
+    grads_there = exchange(1, sent_g, grads)
+    weights_first(1)
+
+    fill_pad(pad, patches_ref[...].astype(F32))
+    conv_into(pad, taps_ref, conv, bias_ref, False)
+    unit, _ = normalise(conv[...])
+    normed[...] = (unit * gain_ref[...] + shift_ref[...]).astype(BF)
+    sent_n[...] = dot(picked[...], normed[...], NN).astype(BF)
+    rows_there = exchange(0, sent_n, rows)
 
     mine = pl.ds(pl.multiple_of(dp * depth, 16), depth)
     win[mine] = w_in_ref[...]
     wout[mine] = w_out_ref[...]
-    all_n[ex] = normed[...]
-    all_c[ex] = cot_ref[...]
-    all_m[ex] = meta[...]
-    for k in range(1, max(chips, 2)):
-        if k < chips:
-            send_step(1, k)
-        if k == 1:
-            weights_on(0)
-        if k < chips:
-            send_step(0, k)
-        if k == 1:
-            weights_on(1)
-    for copy in metas:
-        copy.wait()
-
-    slots = lax.broadcasted_iota(jnp.int32, (cap, tokens), 0).astype(F32) + (ex * cap).astype(F32)
-
-    def choose(j):
-        info = all_m[j]
-        hits = [jnp.where(slots == info[k : k + 1, :], 1.0, 0.0) for k in range(TOP)]
-        weighed = hits[0] * info[TOP : TOP + 1, :]
-        for k in range(1, TOP):
-            weighed = weighed + hits[k] * info[TOP + k : TOP + k + 1, :]
-        select = hits[0]
-        for k in range(1, TOP):
-            select = select + hits[k]
-        return select.astype(BF), jnp.sum(weighed, axis=1, keepdims=True)
-
-    finish_twins(1)
-
-    def gather_grads(j, carry):
-        select, gate = choose(j)
-        at = pl.ds(pl.multiple_of(j * cap, 16), cap)
-        grads[at] = (dot(select, all_c[j], NN) * gate).astype(BF)
-        return carry
-
-    lax.fori_loop(0, n_exp, gather_grads, 0)
-    finish_twins(0)
-
-    def gather_rows(j, carry):
-        select, _ = choose(j)
-        at = pl.ds(pl.multiple_of(j * cap, 16), cap)
-        rows[at] = dot(select, all_n[j], NN).astype(BF)
-        return carry
-
-    lax.fori_loop(0, n_exp, gather_rows, 0)
+    weights_on(0)
+    weights_on(1)
+    for copy in rows_there:
+        copy.wait_recv()
     weights_done(0)
 
     def up(n, carry):
@@ -478,25 +369,9 @@
 
     lax.fori_loop(0, width // tile, down, 0)
 
-    my_rows = pl.ds(pl.multiple_of(ex * cap, 16), cap)
-
-    def give_back(a, src, dst):
-        copies = []
-        for i in range(1, n_exp):
-            to = (ex + i) % n_exp
-            copy = remote(
-                src.at[pl.ds(pl.multiple_of(to * cap, 16), cap)],
-                dst.at[my_rows],
-                ret_send.at[a, i],
-                ret_recv.at[a, i],
-                (dp, to),
-            )
-            copy.start()
-            copies.append(copy)
-        dst[my_rows] = src[my_rows]
-        return copies
-
-    outs_back = give_back(0, outs, r_outs)
+    outs_back = exchange(2, outs, r_outs)
+    for copy in grads_there:
+        copy.wait_recv()
     weight_grad(1, grads, hidden)
 
     def down_grad(n, carry):
@@ -512,27 +387,22 @@
         return carry
 
     lax.fori_loop(0, width // tile, up_grad, 0)
-    grads_back = give_back(1, back, r_back)
+    grads_back = exchange(3, back, r_back)
     weight_grad(0, rows, ghid)
     second_shares(1)
 
-    tall = lax.broadcasted_iota(jnp.int32, (count, tokens), 0).astype(F32)
-    ones = [jnp.where(tall == meta[k : k + 1, :], 1.0, 0.0).astype(BF) for k in range(TOP)]
     for copy in outs_back:
         copy.wait()
-    combined = dot(ones[0], r_outs[...], TN) * gate_ref[:, 0:1]
+    combined = dot(single[0], r_outs[...], TN) * gate_ref[:, 0:1]
     for k in range(1, TOP):
-        combined = combined + dot(ones[k], r_outs[...], TN) * gate_ref[:, k : k + 1]
+        combined = combined + dot(single[k], r_outs[...], TN) * gate_ref[:, k : k + 1]
     mixed_ref[...] = (patches_ref[...].astype(F32) + combined).astype(BF)
     second_shares(0)
 
     for copy in grads_back:
         copy.wait()
-    both = ones[0]
-    for k in range(1, TOP):
-        both = both + ones[k]
     unit, scale = normalise(conv[...])
-    lean = dot(both, r_back[...], TN) * gain_ref[...]
+    lean = dot(picked[...], r_back[...], TN) * gain_ref[...]
     inner = lean - jnp.mean(lean, axis=1, keepdims=True)
     inner = inner - unit * jnp.mean(lean * unit, axis=1, keepdims=True)
     fill_pad(pad, inner * scale)
@@ -541,10 +411,8 @@
 
     weight_sum(1, gw_out_ref)
     weight_sum(0, gw_in_ref)
-    for copy in started + shares:
+    for copy in started + shares + rows_there + grads_there:
         copy.wait_send()
-    finish_sends(0)
-    finish_sends(1)
 
 
 def grid_of(n_dp):
@@ -572,7 +440,6 @@
     count = n_exp * cap
     vmem = pl.BlockSpec(memory_space=pltpu.VMEM)
     dma = pltpu.SemaphoreType.DMA
-    chips = n_exp // 2
     long = max(grid_of(n_dp))
     more = max(long - 1, 1)
     half = depth // 2
@@ -590,13 +457,13 @@
             pltpu.VMEM((IMG_H + 2 * HALF, IMG_W + 2 * EDGE, width), F32),
             pltpu.VMEM((tokens, width), F32),
             pltpu.VMEM((tokens, width), BF),
-            pltpu.VMEM((8, tokens), F32),
             pltpu.VMEM((tokens, 128), F32),
+            pltpu.VMEM((count, width), BF),
+            pltpu.VMEM((count, width), BF),
+            pltpu.VMEM((count, tokens), BF),
+            pltpu.VMEM((TOP, count, tokens), BF),
             pltpu.VMEM((width, hid), BF),
             pltpu.VMEM((width, hid), BF),
-            pltpu.VMEM((n_exp, tokens, width), BF),
-            pltpu.VMEM((n_exp, tokens, width), BF),
-            pltpu.VMEM((n_exp, 8, tokens), F32),
             pltpu.VMEM((count, width), BF),
             pltpu.VMEM((count, width), BF),
             pltpu.VMEM((count, hid), F32),
@@ -613,14 +480,8 @@
             pltpu.VMEM((2, 2, more, half, hid), BF),
             dma((2, 2, long, long)),
             dma((2, 2, long, long)),
-            dma((n_exp,)),
-            dma((n_exp,)),
-            dma((2, 2, chips)),
-            dma((2, 2, chips)),
-            dma((2, 2, chips)),
-            dma((2, 2, chips)),
-            dma((2, n_exp)),
-            dma((2, n_exp)),
+            dma((4, n_exp)),
+            dma((4, n_exp)),
             dma((2, 2, long, long)),
             dma((2, 2, long, long)),
             dma((2, 2, long)),

time: 107 us -> 118 us (1.10)
  Pallas kernels: 97.3 us -> 108 us
    pallas_call x1, Pallas kernels: 97.3 us -> 108 us  [local(): pl.pallas_call(functools.partial(moe_body, n_dp, n_exp, cap), out_shape=(...]
where the time goes in v3:
time: 118 us; the launch traced here: 117 us
  Pallas kernels  108 us (92%)
  local copies, waits for them, and re-layouts  8.37 us (7%)
    pallas_call x1, Pallas kernels, local(): pl.pallas_call(functools.partial(moe_body, n_dp, n_exp, cap), out_shape=(...  108 us
    unnamed x14, local copies, waits for them, and re-layouts  8.37 us

profile of v3, /device:TPU:9, one launch (start us, length us, event | category | flops | bytes accessed | tf_op | source)
XLA Modules:
  0.0 117.5 jit_solution(1616639775076524775)
XLA Ops:
  0.6 0.0 copy-start.2
  0.6 0.7 copy-done.2
  1.3 0.0 copy-start.3
  1.3 0.7 copy.14.ids_ref
  2.1 0.0 copy-done.3
  2.1 0.7 copy.15.gate_ref
  2.8 108.5 %shard_map.129 = (bf16[128,1024]{1,0:T(8,128)(2,1)}, f32[128,1024]{1,0:T(8,128)}, f32[256,1024]{1,0:T(8,128)}, f32[256,1024]{1,0:T(8,128)}) custom-call(bf16[128,1024]{1,0:T(8,128)(2,1)} %patches_ref.1, s32[128,2]{1,0:T(8,128)} %copy.14.ids_ref, f32[128,2]{1,0:T(8,128)} %copy.15.gate_ref, f32[49,1024]{1,0:T(8,128)} %taps_ref.1, f32[1,1024]{1,0:T(1,128)} %bitcast.11, ...), custom_call_target="tpu_custom_call" | custom-call | tf_op jit(solution)/shard_map/pallas_call | solution.py:446
  111.3 0.0 copy-start.1
  111.3 1.8 %copy.20 = bf16[128,1024]{1,0:T(8,128)(2,1)} copy(bf16[128,1024]{1,0:T(8,128)(2,1)} %get-tuple-element.16) | data formatting | bytes 524288
  113.0 1.9 %copy.21 = f32[128,1024]{1,0:T(8,128)} copy(f32[128,1024]{1,0:T(8,128)} %get-tuple-element.17) | data formatting | bytes 1048576
  114.9 0.0 copy-done.1
  114.9 0.0 copy-start
  114.9 1.0 copy.22
  115.9 0.6 copy-done
  116.5 1.0 copy.23
Async XLA Ops:
  0.6 0.7 copy-start.2
  1.3 0.7 copy-start.3
  111.3 3.7 %copy-start.1 = (f32[256,1024]{1,0:T(8,128)S(1)}, f32[256,1024]{1,0:T(8,128)}, u32[]{:S(2)}) copy-start(f32[256,1024]{1,0:T(8,128)} %get-tuple-element.10) | copy-start | bytes 3145732
  114.9 1.6 %copy-start = (f32[256,1024]{1,0:T(8,128)S(1)}, f32[256,1024]{1,0:T(8,128)}, u32[]{:S(2)}) copy-start(f32[256,1024]{1,0:T(8,128)} %get-tuple-element.11) | copy-start | bytes 3145732

commit v4 on v2

--- a/solution.py
+++ b/solution.py
@@ -300,6 +300,8 @@
     unit, _ = normalise(conv[...])
     normed[...] = (unit * gain_ref[...] + shift_ref[...]).astype(BF)
     send_step(0, 0)
+    if chips > 1:
+        send_step(1, 1)
 
     flip[...] = jnp.zeros_like(flip)
     flip[:, 0:TOP] = ids_ref[...].astype(F32)
@@ -335,7 +337,7 @@
     all_c[ex] = cot_ref[...]
     all_m[ex] = meta[...]
     for k in range(1, max(chips, 2)):
-        if k < chips:
+        if 1 < k < chips:
             send_step(1, k)
         if k == 1:
             weights_on(0)

time: 107 us -> 107 us (level)
  no operation moved by 1% of the time
where the time goes in v4:
time: 107 us; the launch traced here: 106 us
  Pallas kernels  97.3 us (91%)
  local copies, waits for them, and re-layouts  8.37 us (8%)
    pallas_call x1, Pallas kernels, local(): pl.pallas_call(functools.partial(moe_body, n_dp, n_exp, cap), out_shape=(...  97.3 us
    unnamed x14, local copies, waits for them, and re-layouts  8.37 us

profile of v4, /device:TPU:9, one launch (start us, length us, event | category | flops | bytes accessed | tf_op | source)
XLA Modules:
  0.0 106.4 jit_solution(3244422444710788924)
XLA Ops:
  0.6 0.0 copy-start.2
  0.6 0.7 copy-done.2
  1.3 0.0 copy-start.3
  1.3 0.7 copy.14.ids_ref
  2.1 0.0 copy-done.3
  2.1 0.7 copy.15.gate_ref
  2.8 97.3 %shard_map.129 = (bf16[128,1024]{1,0:T(8,128)(2,1)}, f32[128,1024]{1,0:T(8,128)}, f32[256,1024]{1,0:T(8,128)}, f32[256,1024]{1,0:T(8,128)}) custom-call(bf16[128,1024]{1,0:T(8,128)(2,1)} %patches_ref.1, s32[128,2]{1,0:T(8,128)} %copy.14.ids_ref, f32[128,2]{1,0:T(8,128)} %copy.15.gate_ref, f32[49,1024]{1,0:T(8,128)} %taps_ref.1, f32[1,1024]{1,0:T(1,128)} %bitcast.11, ...), custom_call_target="tpu_custom_call" | custom-call | tf_op jit(solution)/shard_map/pallas_call | solution.py:581
  100.1 0.0 copy-start.1
  100.1 1.8 %copy.20 = bf16[128,1024]{1,0:T(8,128)(2,1)} copy(bf16[128,1024]{1,0:T(8,128)(2,1)} %get-tuple-element.16) | data formatting | bytes 524288
  101.9 1.9 %copy.21 = f32[128,1024]{1,0:T(8,128)} copy(f32[128,1024]{1,0:T(8,128)} %get-tuple-element.17) | data formatting | bytes 1048576
  103.8 0.0 copy-done.1
  103.8 0.0 copy-start
  103.8 1.0 copy.22
  104.8 0.6 copy-done
  105.4 1.0 copy.23
Async XLA Ops:
  0.6 0.7 copy-start.2
  1.3 0.7 copy-start.3
  100.1 3.7 %copy-start.1 = (f32[256,1024]{1,0:T(8,128)S(1)}, f32[256,1024]{1,0:T(8,128)}, u32[]{:S(2)}) copy-start(f32[256,1024]{1,0:T(8,128)} %get-tuple-element.10) | copy-start | bytes 3145732
  103.8 1.6 %copy-start = (f32[256,1024]{1,0:T(8,128)S(1)}, f32[256,1024]{1,0:T(8,128)}, u32[]{:S(2)}) copy-start(f32[256,1024]{1,0:T(8,128)} %get-tuple-element.11) | copy-start | bytes 3145732
